TPU v7x, 256 devices: a whole 4x4x8 slice. The times are simulated.
256 devices in a mesh: wide: 128 (over x, y_hi, z, core), narrow: 2 (over y_lo).
Axes of the slice: x: 4, y: 4 (y_hi: 2, y_lo: 2; y = y_hi * 2 + y_lo), z: 8, core: 2. Of those that a mesh axis runs over, the one named last changes fastest.
Arguments:
- functions: bfloat16 [1024, 65536], P(('wide', 'narrow')), may hold values from -6 to 6
- potential: float32 [64, 1024], replicated, may hold values from 0 to 2
- cheb_coef: float32 [9], replicated, may hold values from -1 to 1
- block_cols: int32 [16, 12], replicated, may hold values from 0 to 15, all different within a row
- kernel_halves: bfloat16 [2, 16, 12, 2048], P('narrow'), may hold values from -0.21875 to 0.21875
Outputs:
- updated_functions: bfloat16 [1024, 65536], P(('wide', 'narrow'))
Inputs may be any that keep to these rules, and one draw needn't show every extreme that they name: `block_cols`: each block row names 12 different column blocks, and every column block is named by some block row.
All inputs are finite; a program needn't handle non-finite values.
Results may differ from a plain program's by a relative error of at most 0.0071.
Values may be sent and summed in bfloat16 or wider, within the bound.
No kernel may reach another device: no remote copies, remote signals or barrier semaphores. Data moves between devices by JAX's collectives and lax.ppermute only.
A program may use at most 64 MiB of HBM per device.

v0:
```python
import functools

import jax
import jax.numpy as jnp
from jax import lax
from jax.experimental import pallas as pl
from jax.experimental.pallas import tpu as pltpu
from jax.sharding import PartitionSpec as P

FUN_DEV = 4
BOX_X = 64
PLANE = 1024
BLOCK = 64
DEGREE = 8
UPDATES = 2
GRID = 65536
FUNCS = 1024
LANES = 128
SUBLANES = 8
X_IN = BOX_X // SUBLANES
Y_OUT = PLANE // LANES
TILES = GRID // LANES


def filter_kernel(coef_ref, potential_ref, in_ref, out_ref, wide_ref, plane_ref, shift_ref, field_ref, even_ref, odd_ref):
    lane = lax.broadcasted_iota(jnp.int32, (SUBLANES, LANES), 1)
    row = lax.broadcasted_iota(jnp.int32, (SUBLANES, LANES), 0)
    z = lane % 32
    wide_ref[...] = in_ref[...].astype(jnp.float32)
    for yo in range(Y_OUT):
        plane_ref[yo * BOX_X:(yo + 1) * BOX_X, :] = potential_ref[:, yo * LANES:(yo + 1) * LANES]
    for xi in range(X_IN):
        for yo in range(Y_OUT):
            potential = plane_ref[pl.ds(yo * BOX_X + xi, SUBLANES, stride=X_IN), :]
            shift_ref[xi, yo] = 0.5 * (potential - 1.0)

    def stencil_step(source, target, coefficient, last, first):
        zero = jnp.zeros((SUBLANES, LANES), jnp.float32)
        for xi in range(X_IN):
            line = [source[xi, yo] for yo in range(Y_OUT)]
            up = [pltpu.roll(v, 96, 1) for v in line] + [zero]
            down = [zero] + [pltpu.roll(v, 32, 1) for v in line]
            for yo in range(Y_OUT):
                v = line[yo]
                if xi < X_IN - 1:
                    right = source[xi + 1, yo]
                else:
                    right = jnp.where(row < SUBLANES - 1, pltpu.roll(source[0, yo], SUBLANES - 1, 0), 0.0)
                if xi > 0:
                    left = source[xi - 1, yo]
                else:
                    left = jnp.where(row > 0, pltpu.roll(source[X_IN - 1, yo], 1, 0), 0.0)
                total = left + right
                total = total + jnp.where(lane < 96, up[yo], up[yo + 1])
                total = total + jnp.where(lane >= 32, down[yo + 1], down[yo])
                total = total + jnp.where(z < 31, pltpu.roll(v, 127, 1), 0.0)
                total = total + jnp.where(z > 0, pltpu.roll(v, 1, 1), 0.0)
                applied = shift_ref[xi, yo] * v - 0.25 * total
                if last:
                    applied = 0.5 * applied
                value = coefficient * field_ref[xi, yo] + applied
                if not first:
                    value = value - target[xi, yo]
                target[xi, yo] = value

    def one_function(fun, carry):
        for xi in range(X_IN):
            for yo in range(Y_OUT):
                start = (xi * Y_OUT + yo) * FUN_DEV + fun
                field_ref[xi, yo] = wide_ref[pl.ds(start, SUBLANES, stride=X_IN * Y_OUT * FUN_DEV), :]

        def one_update(update, carry):
            for xi in range(X_IN):
                for yo in range(Y_OUT):
                    even_ref[xi, yo] = coef_ref[DEGREE] * field_ref[xi, yo]
            source, target = even_ref, odd_ref
            for order in range(DEGREE - 1, -1, -1):
                stencil_step(source, target, coef_ref[order], order == 0, order == DEGREE - 1)
                source, target = target, source
            for xi in range(X_IN):
                for yo in range(Y_OUT):
                    field_ref[xi, yo] = source[xi, yo]
            return carry

        lax.fori_loop(0, UPDATES, one_update, 0)
        for xi in range(X_IN):
            for yo in range(Y_OUT):
                start = (xi * Y_OUT + yo) * FUN_DEV + fun
                wide_ref[pl.ds(start, SUBLANES, stride=X_IN * Y_OUT * FUN_DEV), :] = field_ref[xi, yo]
        return carry

    lax.fori_loop(0, FUN_DEV, one_function, 0)
    out_ref[...] = wide_ref[...].astype(jnp.bfloat16)


def filter_twice(rows, potential, coefficient):
    vectors = pltpu.VMEM((X_IN, Y_OUT, SUBLANES, LANES), jnp.float32)
    return pl.pallas_call(
        filter_kernel,
        name="filter_twice",
        out_shape=jax.ShapeDtypeStruct(rows.shape, jnp.bfloat16),
        in_specs=[
            pl.BlockSpec(memory_space=pltpu.SMEM),
            pl.BlockSpec(memory_space=pltpu.VMEM),
            pl.BlockSpec(memory_space=pltpu.VMEM),
        ],
        out_specs=pl.BlockSpec(memory_space=pltpu.VMEM),
        scratch_shapes=[pltpu.VMEM(rows.shape, jnp.float32), pltpu.VMEM((BOX_X * Y_OUT, LANES), jnp.float32), vectors, vectors, vectors, vectors],
        compiler_params=pltpu.CompilerParams(vmem_limit_bytes=16 * 2**20),
        cost_estimate=pl.CostEstimate(flops=60_000_000, bytes_accessed=40_000_000, transcendentals=0),
    )(coefficient, potential, rows)


def mix_kernel(mixer_ref, points_ref, out_ref, middle_ref):
    middle_ref[...] = jnp.dot(
        mixer_ref[...], points_ref[...], preferred_element_type=jnp.float32
    ).astype(jnp.bfloat16)
    out_ref[...] = jnp.dot(
        mixer_ref[...], middle_ref[...], preferred_element_type=jnp.float32
    ).astype(jnp.bfloat16)


def mix_twice(mixer, points):
    return pl.pallas_call(
        mix_kernel,
        name="mix_twice",
        out_shape=jax.ShapeDtypeStruct(points.shape, jnp.bfloat16),
        in_specs=[pl.BlockSpec(memory_space=pltpu.VMEM)] * 2,
        out_specs=pl.BlockSpec(memory_space=pltpu.VMEM),
        scratch_shapes=[pltpu.VMEM(points.shape, jnp.bfloat16)],
        compiler_params=pltpu.CompilerParams(vmem_limit_bytes=24 * 2**20),
        cost_estimate=pl.CostEstimate(flops=1_100_000_000, bytes_accessed=4_000_000, transcendentals=0),
    )(mixer, points)


def dense_mixer(halves, block_cols):
    row_blocks, slots = block_cols.shape
    chosen = (block_cols[:, :, None] == jnp.arange(row_blocks)[None, None, :]).astype(jnp.bfloat16)
    spread = jnp.einsum("rsb,prsk->prbk", chosen, halves, preferred_element_type=jnp.float32).astype(jnp.bfloat16)
    spread = spread.reshape(2, row_blocks, row_blocks, BLOCK // (2 * FUN_DEV), 2, FUN_DEV, BLOCK // 2)
    return spread.transpose(4, 1, 3, 5, 0, 2, 6).reshape(FUNCS, FUNCS)


def local(functions, potential, cheb_coef, block_cols, kernel_halves):
    devices = lax.axis_size("wide") * lax.axis_size("narrow")
    own = GRID // devices
    halves = lax.all_gather(kernel_halves, "narrow", axis=0, tiled=True)
    mixer = dense_mixer(halves, block_cols)
    rows = functions.reshape(FUN_DEV, TILES, LANES).transpose(1, 0, 2).reshape(TILES * FUN_DEV, LANES)
    filtered = filter_twice(rows, potential, cheb_coef)
    outgoing = filtered.reshape(devices, own // LANES, FUN_DEV, LANES).transpose(0, 2, 1, 3)
    outgoing = outgoing.reshape(devices, FUN_DEV, own)
    points = lax.all_to_all(outgoing, ("narrow", "wide"), split_axis=0, concat_axis=0, tiled=True)
    mixed = mix_twice(mixer, points.reshape(FUNCS, own))
    result = lax.all_to_all(
        mixed.reshape(devices, FUN_DEV, own), ("narrow", "wide"), split_axis=0, concat_axis=0, tiled=True
    )
    return result.transpose(1, 0, 2).reshape(FUN_DEV, GRID)


def solution(mesh):
    return jax.shard_map(
        local,
        mesh=mesh,
        in_specs=(P(("wide", "narrow"), None), P(), P(), P(), P("narrow", None, None, None)),
        out_specs=P(("wide", "narrow"), None),
        check_vma=False,
    )
```

profile of v0, /device:TPU:1, one launch (start us, length us, event | category | flops | bytes accessed | tf_op | source)
XLA Modules:
  0.0 140.2 jit_solution(8550524739911681811)
XLA Ops:
  6.5 0.0 copy-start
  6.5 0.0 copy-start.1
  6.5 0.0 copy-start.2
  6.5 0.0 all-gather.2.cloned.1.call-start
  6.5 2.7 %copy.6 = bf16[1,16,12,2048]{3,2,0,1:T(8,128)(2,1)} copy(bf16[1,16,12,2048]{3,1,2,0:T(8,128)(2,1)} %param.9) | data formatting | bytes 1572864 | tf_op args[4]
  9.2 0.0 copy-start.3
  9.2 0.0 all-gather.2.cloned.1.call-update
  9.2 0.0 copy-done
  9.2 0.0 copy-done.1
  9.3 0.0 copy-done.2
  9.3 20.0 %filter_twice.1 = bf16[2048,128]{1,0:T(8,128)(2,1)S(1)} custom-call(f32[9]{0:T(128)S(1)} %copy-done.2, f32[64,1024]{1,0:T(8,128)S(1)} %copy-done.1, bf16[2048,128]{1,0:T(8,128)(2,1)S(1)} %bitcast.31), custom_call_target="tpu_custom_call" | custom-call | flops 60000000 | bytes 40000000 | tf_op jit(solution)/shard_map/filter_twice/pallas_call | solution.py:98
  29.2 35.9 %all_to_all.10 = bf16[256,4,256]{2,1,0:T(4,128)(2,1)S(1)} all-to-all(bf16[256,4,256]{2,1,0:T(4,128)(2,1)S(1)} %bitcast.30), channel_id=1, replica_groups=mesh['wide'=128,'narrow'=2] {'narrow','wide'}, dimensions={0} | all-to-all | bytes 1048576 | tf_op jit(solution)/shard_map/all_to_all | solution.py:153
  65.1 0.1 reshape.34.points_ref
  65.3 0.0 all-gather.2.cloned.1.call-done
  65.3 0.0 copy-done.3
  65.3 2.3 %fusion = bf16[2,16,16,2048]{3,2,0,1:T(8,128)(2,1)S(1)} fusion(bf16[2,16,12,2048]{3,2,0,1:T(8,128)(2,1)} %all-gather.2.cloned.1.call-done, s32[16,12]{1,0:T(8,128)S(1)} %copy-done.3), kind=kOutput, calls=%fused_computation.2 | convolution fusion | flops 26217472 | bytes 3670784 | tf_op jit(solution)/shard_map/rsb,prsk->prbk/dot_general | solution.py:139
  67.6 8.1 %reshape.28 = bf16[2,16,16,8,2,4,32]{6,5,4,3,2,0,1:T(4,128)(2,1)} reshape(bf16[2,16,16,2048]{3,2,0,1:T(8,128)(2,1)S(1)} %fusion) | data formatting | bytes 4194304 | tf_op jit(solution)/shard_map/reshape | solution.py:140
  75.7 16.3 %copy.12 = bf16[2,16,16,8,2,4,32]{6,2,0,5,3,1,4:T(8,128)(2,1)} copy(bf16[2,16,16,8,2,4,32]{6,5,4,3,2,0,1:T(4,128)(2,1)} %reshape.28) | data formatting | bytes 4194304 | tf_op jit(solution)/shard_map/reshape | solution.py:140
  92.0 11.3 %reshape.29.mixer_ref = bf16[1024,1024]{1,0:T(8,128)(2,1)S(1)} reshape(bf16[2,16,8,4,2,16,32]{6,5,4,3,2,1,0:T(8,128)(2,1)} %bitcast.32) | data formatting | bytes 4194304 | tf_op jit(solution)/shard_map/reshape | solution.py:141
  103.3 2.2 %mix_twice.1 = bf16[1024,256]{1,0:T(8,128)(2,1)S(1)} custom-call(bf16[1024,1024]{1,0:T(8,128)(2,1)S(1)} %reshape.29.mixer_ref, bf16[1024,256]{1,0:T(8,128)(2,1)S(1)} %reshape.34.points_ref), custom_call_target="tpu_custom_call" | custom-call | flops 1100000000 | bytes 4000000 | tf_op jit(solution)/shard_map/mix_twice/pallas_call | solution.py:124
  105.5 0.1 reshape.35
  105.7 26.9 %all_to_all.11 = bf16[256,4,256]{2,1,0:T(4,128)(2,1)S(1)} all-to-all(bf16[256,4,256]{2,1,0:T(4,128)(2,1)S(1)} %reshape.35), channel_id=1, replica_groups=mesh['wide'=128,'narrow'=2] {'narrow','wide'}, dimensions={0} | all-to-all | bytes 1048576 | tf_op jit(solution)/shard_map/all_to_all | solution.py:155
  132.5 0.8 copy.14
Async XLA Ops:
  6.5 2.7 %copy-start = (bf16[4,65536]{1,0:T(4,128)(2,1)S(1)}, bf16[4,65536]{1,0:T(4,128)(2,1)}, u32[]{:S(2)}) copy-start(bf16[4,65536]{1,0:T(4,128)(2,1)} %param.5) | copy-start | bytes 1572868
  6.5 2.7 %copy-start.1 = (f32[64,1024]{1,0:T(8,128)S(1)}, f32[64,1024]{1,0:T(8,128)}, u32[]{:S(2)}) copy-start(f32[64,1024]{1,0:T(8,128)} %potential_ref.1) | copy-start | bytes 786436
  6.5 2.7 %copy-start.2 = (f32[9]{0:T(128)S(1)}, f32[9]{0:T(128)}, u32[]{:S(2)}) copy-start(f32[9]{0:T(128)} %coef_ref.1) | copy-start | bytes 112
  6.5 58.7 %all-gather.2.cloned.1.call-start = ((), (), s32[]{:S(2)}) async-start(), calls=%async_computation.2 | async-start | bytes 3145728 | tf_op jit(solution)/shard_map/all_gather | solution.py:147
  9.2 56.1 %copy-start.3 = (s32[16,12]{1,0:T(8,128)S(1)}, s32[16,12]{1,0:T(8,128)}, u32[]{:S(2)}) copy-start(s32[16,12]{1,0:T(8,128)} %param.8) | copy-start | bytes 2308
Sparse Core Ops, SparseCore 0:
  9.4 44.1 all-gather.1
where the time goes:
time: 141 us; the launch traced here: 140 us
  blocking collectives  62.8 us (45%)
  local copies, waits for them, and re-layouts  39.4 us (28%)
  Pallas kernels  22.2 us (16%)
  between operations  13.5 us (10%)
  matrix products  2.28 us (2%)
    all_to_all x1, blocking collectives, local(): lax.all_to_all(outgoing, ('narrow', 'wide'), split_axis=0, concat_axis=0,...  35.9 us
    all_to_all x1, blocking collectives, local(): lax.all_to_all(mixed.reshape(devices, FUN_DEV, own), ('narrow', 'wide'),...  26.9 us
    reshape x2, local copies, waits for them, and re-layouts, dense_mixer(): spread.reshape(2, row_blocks, row_blocks, BLOCK // (2 * FUN_DEV), 2, FUN_...  24.4 us
    pallas_call x1, Pallas kernels, filter_twice(): pl.pallas_call(filter_kernel, name='filter_twice', out_shape=jax.ShapeDty...  20 us
    reshape x1, local copies, waits for them, and re-layouts, dense_mixer(): return spread.transpose(4, 1, 3, 5, 0, 2, 6).reshape(FUNCS, FUNCS)  11.3 us
    unnamed x10, local copies, waits for them, and re-layouts  3.47 us
  transfers between devices with their start and end apart: 1, of which 0 were waited for; matrix products, arithmetic and copies ran while one was open for 0% of the time, Pallas kernels for 14%

commit v1 on v0

--- a/solution.py
+++ b/solution.py
@@ -1,5 +1,3 @@
-import functools
-
 import jax
 import jax.numpy as jnp
 from jax import lax
@@ -9,7 +7,8 @@
 
 FUN_DEV = 4
 BOX_X = 64
-PLANE = 1024
+BOX_Y = 32
+BOX_Z = 32
 BLOCK = 64
 DEGREE = 8
 UPDATES = 2
@@ -18,8 +17,22 @@
 LANES = 128
 SUBLANES = 8
 X_IN = BOX_X // SUBLANES
-Y_OUT = PLANE // LANES
+Y_OUT = BOX_Y * BOX_Z // LANES
 TILES = GRID // LANES
+
+
+def swap_chunks(group, lane):
+    low = lane < 64
+    even = (lane // 32) % 2 == 0
+    upper, lower = [], []
+    for first, second in ((group[0], group[2]), (group[1], group[3])):
+        upper.append(jnp.where(low, first, pltpu.roll(second, 64, 1)))
+        lower.append(jnp.where(low, pltpu.roll(first, 64, 1), second))
+    out = []
+    for first, second in (upper, lower):
+        out.append(jnp.where(even, first, pltpu.roll(second, 32, 1)))
+        out.append(jnp.where(even, pltpu.roll(first, 96, 1), second))
+    return out
 
 
 def filter_kernel(coef_ref, potential_ref, in_ref, out_ref, wide_ref, plane_ref, shift_ref, field_ref, even_ref, odd_ref):
@@ -133,21 +146,85 @@
     )(mixer, points)
 
 
-def dense_mixer(halves, block_cols):
+def spread_kernel(half_ref, place_ref, own_ref, other_ref, out_ref, wide_ref):
+    lane = lax.broadcasted_iota(jnp.int32, (SUBLANES, LANES), 1)
+    row_blocks = FUNCS // BLOCK
+    column_tiles = FUNCS // 2 // LANES
+    for source_ref, half in ((own_ref, half_ref[0]), (other_ref, 1 - half_ref[0])):
+        def one_pair(pair, carry, source_ref=source_ref, half=half):
+            spread = jnp.dot(
+                place_ref[...],
+                source_ref[:, pl.ds(pl.multiple_of(pair * 2 * LANES, 2 * LANES), 2 * LANES)],
+                preferred_element_type=jnp.float32,
+            )
+            for side in range(2):
+                for tile in range(column_tiles):
+                    for rows in range(row_blocks // SUBLANES):
+                        group = [
+                            spread[
+                                (tile * 4 + step) * row_blocks + rows * SUBLANES:
+                                (tile * 4 + step) * row_blocks + (rows + 1) * SUBLANES,
+                                side * LANES:(side + 1) * LANES,
+                            ]
+                            for step in range(4)
+                        ]
+                        for fun, value in enumerate(swap_chunks(group, lane)):
+                            start = (half * column_tiles + tile) * FUNCS
+                            start = start + side * (FUNCS // 2) + rows * SUBLANES * (BLOCK // 2) + pair * FUN_DEV + fun
+                            wide_ref[pl.ds(start, SUBLANES, stride=BLOCK // 2), :] = value
+            return carry
+
+        lax.fori_loop(0, BLOCK * BLOCK // 2 // (2 * LANES), one_pair, 0)
+    for tile in range(FUNCS // LANES):
+        out_ref[:, tile * LANES:(tile + 1) * LANES] = wide_ref[tile * FUNCS:(tile + 1) * FUNCS, :].astype(jnp.bfloat16)
+
+
+def dense_mixer(half, own, other, block_cols):
     row_blocks, slots = block_cols.shape
-    chosen = (block_cols[:, :, None] == jnp.arange(row_blocks)[None, None, :]).astype(jnp.bfloat16)
-    spread = jnp.einsum("rsb,prsk->prbk", chosen, halves, preferred_element_type=jnp.float32).astype(jnp.bfloat16)
-    spread = spread.reshape(2, row_blocks, row_blocks, BLOCK // (2 * FUN_DEV), 2, FUN_DEV, BLOCK // 2)
-    return spread.transpose(4, 1, 3, 5, 0, 2, 6).reshape(FUNCS, FUNCS)
+    entry = jnp.arange(slots * row_blocks)
+    place = jnp.arange(row_blocks * row_blocks)
+    column = block_cols.T.reshape(-1)
+    chosen = (column[None, :] == place[:, None] // row_blocks) & (
+        entry[None, :] % row_blocks == place[:, None] % row_blocks
+    )
+
+    def flat(blocks):
+        return blocks[0].transpose(1, 0, 2).reshape(slots * row_blocks, BLOCK * BLOCK // 2)
+
+    return pl.pallas_call(
+        spread_kernel,
+        name="spread_blocks",
+        out_shape=jax.ShapeDtypeStruct((FUNCS, FUNCS), jnp.bfloat16),
+        in_specs=[pl.BlockSpec(memory_space=pltpu.SMEM)] + [pl.BlockSpec(memory_space=pltpu.VMEM)] * 3,
+        out_specs=pl.BlockSpec(memory_space=pltpu.VMEM),
+        scratch_shapes=[pltpu.VMEM((FUNCS * FUNCS // LANES, LANES), jnp.float32)],
+        compiler_params=pltpu.CompilerParams(vmem_limit_bytes=16 * 2**20),
+        cost_estimate=pl.CostEstimate(flops=400_000_000, bytes_accessed=15_000_000, transcendentals=0),
+    )(half.reshape(1), chosen.astype(jnp.bfloat16), flat(own), flat(other))
+
+
+def other_half_pairs(wide, narrow):
+    pairs = []
+    for target in range(wide * narrow):
+        rest, low = divmod(target, 2)
+        rest, core = divmod(rest, 2)
+        rest, z = divmod(rest, 8)
+        x, high = divmod(rest, 2)
+        y = (high * 2 + low + (1 if core == 0 else 3)) % 4
+        pairs.append(((((x * 2 + y // 2) * 8 + z) * 2 + core) * 2 + y % 2, target))
+    return pairs
 
 
 def local(functions, potential, cheb_coef, block_cols, kernel_halves):
     devices = lax.axis_size("wide") * lax.axis_size("narrow")
     own = GRID // devices
-    halves = lax.all_gather(kernel_halves, "narrow", axis=0, tiled=True)
-    mixer = dense_mixer(halves, block_cols)
+    other = lax.ppermute(
+        kernel_halves, ("wide", "narrow"), other_half_pairs(lax.axis_size("wide"), lax.axis_size("narrow"))
+    )
     rows = functions.reshape(FUN_DEV, TILES, LANES).transpose(1, 0, 2).reshape(TILES * FUN_DEV, LANES)
     filtered = filter_twice(rows, potential, cheb_coef)
+    filtered, other = lax.optimization_barrier((filtered, other))
+    mixer = dense_mixer(lax.axis_index("narrow"), kernel_halves, other, block_cols)
     outgoing = filtered.reshape(devices, own // LANES, FUN_DEV, LANES).transpose(0, 2, 1, 3)
     outgoing = outgoing.reshape(devices, FUN_DEV, own)
     points = lax.all_to_all(outgoing, ("narrow", "wide"), split_axis=0, concat_axis=0, tiled=True)

time: 141 us -> 90.5 us (0.64)
  blocking collectives: 62.8 us -> 26.9 us
  local copies, waits for them, and re-layouts: 39.4 us -> 4.99 us
  starting transfers between devices: 0.01 us -> 16.2 us
  between operations: 13.5 us -> 0.09 us
  waiting for transfers between devices: 0.04 us -> 10.5 us
  Pallas kernels: 22.2 us -> 31.4 us
  matrix products: 2.28 us -> 0 us
    all_to_all x1 -> x0, blocking collectives: 35.9 us -> none  [local(): lax.all_to_all(outgoing, ('narrow', 'wide'), split_axis=0, concat_axis=0,...]
    reshape x3 -> x0, local copies, waits for them, and re-layouts: 35.7 us -> none  [the longest x2 24.4 us: dense_mixer(): spread.reshape(2, row_blocks, row_blocks, BLOCK // (2 * FUN_DEV), 2, FUN_...]
    all_to_all x0 -> x1, starting transfers between devices: none -> 14.1 us  [local(): lax.all_to_all(outgoing, ('narrow', 'wide'), split_axis=0, concat_axis=0,...]
    all_to_all x0 -> x1, waiting for transfers between devices: none -> 10.5 us  [local(): lax.all_to_all(outgoing, ('narrow', 'wide'), split_axis=0, concat_axis=0,...]
    pallas_call x0 -> x1, Pallas kernels: none -> 8.41 us  [dense_mixer(): pl.pallas_call(spread_kernel, name='spread_blocks', out_shape=jax.ShapeDt...]
    dot_general x1 -> x0, matrix products: 2.28 us -> none  [dense_mixer(): jnp.einsum('rsb,prsk->prbk', chosen, halves, preferred_element_type=jnp.f...]
    ppermute x0 -> x1, starting transfers between devices: none -> 2.13 us  [local(): lax.ppermute(kernel_halves, ('wide', 'narrow'), other_half_pairs(lax.axis...]
    unnamed x10 -> x15, local copies, waits for them, and re-layouts: 3.47 us -> 4.58 us
  transfers between devices with their start and end apart: 1 -> 2, of which waited for: 0 -> 1; matrix products, arithmetic and copies ran while one was open for 0% -> 0% of each run, Pallas kernels for 14% -> 32%
where the time goes in v1:
time: 90.5 us; the launch traced here: 90.2 us
  Pallas kernels  31.4 us (35%)
  blocking collectives  26.9 us (30%)
  starting transfers between devices  16.2 us (18%)
  waiting for transfers between devices  10.5 us (12%)
  local copies, waits for them, and re-layouts  4.99 us (6%)
    all_to_all x1, blocking collectives, local(): lax.all_to_all(mixed.reshape(devices, FUN_DEV, own), ('narrow', 'wide'),...  26.9 us
    pallas_call x1, Pallas kernels, filter_twice(): pl.pallas_call(filter_kernel, name='filter_twice', out_shape=jax.ShapeDty...  20.8 us
    all_to_all x1, starting transfers between devices, local(): lax.all_to_all(outgoing, ('narrow', 'wide'), split_axis=0, concat_axis=0,...  14.1 us
    all_to_all x1, waiting for transfers between devices, local(): lax.all_to_all(outgoing, ('narrow', 'wide'), split_axis=0, concat_axis=0,...  10.5 us
    pallas_call x1, Pallas kernels, dense_mixer(): pl.pallas_call(spread_kernel, name='spread_blocks', out_shape=jax.ShapeDt...  8.41 us
    unnamed x15, local copies, waits for them, and re-layouts  4.58 us
    pallas_call x1, Pallas kernels, mix_twice(): pl.pallas_call(mix_kernel, name='mix_twice', out_shape=jax.ShapeDtypeStru...  2.22 us
    ppermute x1, starting transfers between devices, local(): lax.ppermute(kernel_halves, ('wide', 'narrow'), other_half_pairs(lax.axis...  2.13 us
  transfers between devices with their start and end apart: 2, of which 1 were waited for; matrix products, arithmetic and copies ran while one was open for 0% of the time, Pallas kernels for 32%

profile of v1, /device:TPU:1, one launch (start us, length us, event | category | flops | bytes accessed | tf_op | source)
XLA Modules:
  0.0 90.2 jit_solution(15718505301807635957)
XLA Ops:
  0.0 0.0 copy-start
  0.0 2.1 %collective-permute-start = (bf16[1,16,12,2048]{3,1,2,0:T(8,128)(2,1)}, bf16[1,16,12,2048]{3,1,2,0:T(8,128)(2,1)S(1)}, u32[]{:S(2)}, u32[]{:S(2)}) collective-permute-start(bf16[1,16,12,2048]{3,1,2,0:T(8,128)(2,1)} %param.9), channel_id=1, source_target_pairs={{1,0},{32,1},{35,2},{2,3},{5,4},{36,5},{39,6},{6,7},{9,8},{40,9},{... | collective-permute-start | bytes 2359304 | tf_op jit(solution)/shard_map/ppermute | solution.py:221
  2.1 0.0 copy-start.3
  2.1 1.0 %copy-done.3 = bf16[4,65536]{1,0:T(4,128)(2,1)S(1)} copy-done((bf16[4,65536]{1,0:T(4,128)(2,1)S(1)}, bf16[4,65536]{1,0:T(4,128)(2,1)}, u32[]{:S(2)}) %copy-start.3) | copy-done | bytes 524312
  3.2 0.0 copy-start.4
  3.2 0.9 %copy-done.4 = f32[64,1024]{1,0:T(8,128)S(1)} copy-done((f32[64,1024]{1,0:T(8,128)S(1)}, f32[64,1024]{1,0:T(8,128)}, u32[]{:S(2)}) %copy-start.4) | copy-done | bytes 262168
  4.1 0.0 copy-start.5
  4.1 0.7 copy-done.5
  4.8 0.0 copy-start.6
  4.8 20.8 %filter_twice.1 = bf16[2048,128]{1,0:T(8,128)(2,1)} custom-call(f32[9]{0:T(128)S(1)} %copy-done.5, f32[64,1024]{1,0:T(8,128)S(1)} %copy-done.4, bf16[2048,128]{1,0:T(8,128)(2,1)S(1)} %bitcast.27), custom_call_target="tpu_custom_call" | custom-call | flops 60000000 | bytes 40000000 | tf_op jit(solution)/shard_map/filter_twice/pallas_call | solution.py:111
  25.5 0.0 collective-permute-done
  25.5 0.0 copy-start.1
  25.5 14.1 %all-to-all-start = ((bf16[256,4,256]{2,1,0:T(4,128)(2,1)}), bf16[256,4,256]{2,1,0:T(4,128)(2,1)S(1)}, u32[]{:S(2)}, u32[]{:S(2)}) async-start(bf16[256,4,256]{2,1,0:T(4,128)(2,1)} %bitcast.13), calls=%async_computation | async-start | bytes 1048576 | tf_op jit(solution)/shard_map/all_to_all | solution.py:230
  39.6 0.0 copy-done.6
  39.7 0.1 copy.8
  39.7 0.1 eq.32
  39.8 0.1 and_convert_fusion.place_ref
  40.0 0.0 copy-done.1
  40.0 0.0 copy-done
  40.0 0.0 copy-start.2
  40.0 1.1 %copy-done.2 = bf16[1,16,12,2048]{3,1,2,0:T(8,128)(2,1)S(1)} copy-done((bf16[1,16,12,2048]{3,1,2,0:T(8,128)(2,1)S(1)}, bf16[1,16,12,2048]{3,1,2,0:T(8,128)(2,1)}, u32[]{:S(2)}) %copy-start.2) | copy-done | bytes 786456
  41.1 8.4 %spread_blocks.1.mixer_ref = bf16[1024,1024]{1,0:T(8,128)(2,1)S(1)} custom-call(s32[1]{0:T(128)} %bitcast.half_ref, bf16[256,192]{1,0:T(8,128)(2,1)S(1)} %and_convert_fusion.place_ref, bf16[192,2048]{1,0:T(8,128)(2,1)S(1)} %bitcast.25, bf16[192,2048]{1,0:T(8,128)(2,1)S(1)} %bitcast.26), custom_call_target="tpu_custom_call" | custom-call | flops 400000000 | bytes 15000000 | tf_op jit(solution)/shard_map/spread_blocks/pallas_call | solution.py:194
  49.6 10.5 %all-to-all-done = bf16[256,4,256]{2,1,0:T(4,128)(2,1)S(1)} async-done(((bf16[256,4,256]{2,1,0:T(4,128)(2,1)}), bf16[256,4,256]{2,1,0:T(4,128)(2,1)S(1)}, u32[]{:S(2)}, u32[]{:S(2)}) %all-to-all-start) | async-done | bytes 524320 | tf_op jit(solution)/shard_map/all_to_all | solution.py:230
  60.1 0.1 reshape.105.points_ref
  60.2 2.2 %mix_twice.1 = bf16[1024,256]{1,0:T(8,128)(2,1)S(1)} custom-call(bf16[1024,1024]{1,0:T(8,128)(2,1)S(1)} %spread_blocks.1.mixer_ref, bf16[1024,256]{1,0:T(8,128)(2,1)S(1)} %reshape.105.points_ref), custom_call_target="tpu_custom_call" | custom-call | flops 1100000000 | bytes 4000000 | tf_op jit(solution)/shard_map/mix_twice/pallas_call | solution.py:137
  62.4 0.1 reshape.106
  62.6 26.9 %all_to_all.10 = bf16[256,4,256]{2,1,0:T(4,128)(2,1)S(1)} all-to-all(bf16[256,4,256]{2,1,0:T(4,128)(2,1)S(1)} %reshape.106), channel_id=1, replica_groups=mesh['wide'=128,'narrow'=2] {'narrow','wide'}, dimensions={0} | all-to-all | bytes 1048576 | tf_op jit(solution)/shard_map/all_to_all | solution.py:232
  89.4 0.8 copy.12
  (2 shorter events, 0.0 us)
Async XLA Ops:
  0.0 40.0 %copy-start = (bf16[1,16,12,2048]{3,1,2,0:T(8,128)(2,1)S(1)}, bf16[1,16,12,2048]{3,1,2,0:T(8,128)(2,1)}, u32[]{:S(2)}) copy-start(bf16[1,16,12,2048]{3,1,2,0:T(8,128)(2,1)} %param.9) | copy-start | bytes 2359300
  0.0 25.5 %collective-permute-start = (bf16[1,16,12,2048]{3,1,2,0:T(8,128)(2,1)}, bf16[1,16,12,2048]{3,1,2,0:T(8,128)(2,1)S(1)}, u32[]{:S(2)}, u32[]{:S(2)}) collective-permute-start(bf16[1,16,12,2048]{3,1,2,0:T(8,128)(2,1)} %param.9), channel_id=1, source_target_pairs={{1,0},{32,1},{35,2},{2,3},{5,4},{36,5},{39,6},{6,7},{9,8},{40,9},{... | collective-permute-start | bytes 2359304 | tf_op jit(solution)/shard_map/ppermute | solution.py:221
  2.1 1.0 %copy-start.3 = (bf16[4,65536]{1,0:T(4,128)(2,1)S(1)}, bf16[4,65536]{1,0:T(4,128)(2,1)}, u32[]{:S(2)}) copy-start(bf16[4,65536]{1,0:T(4,128)(2,1)} %param.5) | copy-start | bytes 1572868
  3.2 0.9 %copy-start.4 = (f32[64,1024]{1,0:T(8,128)S(1)}, f32[64,1024]{1,0:T(8,128)}, u32[]{:S(2)}) copy-start(f32[64,1024]{1,0:T(8,128)} %potential_ref.1) | copy-start | bytes 786436
  4.1 0.7 copy-start.5
  4.8 34.9 %copy-start.6 = (s32[16,12]{1,0:T(8,128)S(1)}, s32[16,12]{1,0:T(8,128)}, u32[]{:S(2)}) copy-start(s32[16,12]{1,0:T(8,128)} %param.8) | copy-start | bytes 2308
  25.5 14.4 %copy-start.1 = (bf16[1,16,12,2048]{3,1,2,0:T(8,128)(2,1)}, bf16[1,16,12,2048]{3,1,2,0:T(8,128)(2,1)S(1)}, u32[]{:S(2)}) copy-start(bf16[1,16,12,2048]{3,1,2,0:T(8,128)(2,1)S(1)} %collective-permute-done) | copy-start | bytes 2359300
  25.5 34.5 %all-to-all-start = ((bf16[256,4,256]{2,1,0:T(4,128)(2,1)}), bf16[256,4,256]{2,1,0:T(4,128)(2,1)S(1)}, u32[]{:S(2)}, u32[]{:S(2)}) async-start(bf16[256,4,256]{2,1,0:T(4,128)(2,1)} %bitcast.13), calls=%async_computation | async-start | bytes 1048576 | tf_op jit(solution)/shard_map/all_to_all | solution.py:230
  40.0 1.1 %copy-start.2 = (bf16[1,16,12,2048]{3,1,2,0:T(8,128)(2,1)S(1)}, bf16[1,16,12,2048]{3,1,2,0:T(8,128)(2,1)}, u32[]{:S(2)}) copy-start(bf16[1,16,12,2048]{3,1,2,0:T(8,128)(2,1)} %copy-done.1) | copy-start | bytes 2359300

commit v2 on v1

--- a/solution.py
+++ b/solution.py
@@ -16,7 +16,9 @@
 FUNCS = 1024
 LANES = 128
 SUBLANES = 8
-X_IN = BOX_X // SUBLANES
+X_FAR = 2
+X_IN = 8
+PARTS = 16
 Y_OUT = BOX_Y * BOX_Z // LANES
 TILES = GRID // LANES
 
@@ -35,98 +37,180 @@
     return out
 
 
-def filter_kernel(coef_ref, potential_ref, in_ref, out_ref, wide_ref, plane_ref, shift_ref, field_ref, even_ref, odd_ref):
+def point_order(size):
+    first = lax.broadcasted_iota(jnp.int32, (size, size), 0)
+    second = lax.broadcasted_iota(jnp.int32, (size, size), 1)
+    column = first // 32 * 32 + first % 8 * 4 + first // 8 % 4
+    return (second == column).astype(jnp.float32).astype(jnp.bfloat16)
+
+
+def filter_kernel(
+    coef_hbm,
+    potential_hbm,
+    in_hbm,
+    out_ref,
+    coef_ref,
+    potential_ref,
+    in_ref,
+    plane_ref,
+    turned_ref,
+    shift_ref,
+    field_ref,
+    even_ref,
+    odd_ref,
+    semaphores,
+):
+    arrivals = [
+        pltpu.make_async_copy(source, target, semaphores.at[index])
+        for index, (source, target) in enumerate(
+            ((potential_hbm, potential_ref), (in_hbm, in_ref), (coef_hbm, coef_ref))
+        )
+    ]
+    for arrival in arrivals:
+        arrival.start()
     lane = lax.broadcasted_iota(jnp.int32, (SUBLANES, LANES), 1)
     row = lax.broadcasted_iota(jnp.int32, (SUBLANES, LANES), 0)
-    z = lane % 32
-    wide_ref[...] = in_ref[...].astype(jnp.float32)
+    y_out = (lane // FUN_DEV) % Y_OUT
+    order_z = point_order(LANES)
+    first = lax.broadcasted_iota(jnp.int32, (LANES, LANES), 0)
+    second = lax.broadcasted_iota(jnp.int32, (LANES, LANES), 1)
+    unit = (first == second).astype(jnp.float32).astype(jnp.bfloat16)
+    x_rows = Y_OUT * FUN_DEV
+
+    arrivals[0].wait()
     for yo in range(Y_OUT):
-        plane_ref[yo * BOX_X:(yo + 1) * BOX_X, :] = potential_ref[:, yo * LANES:(yo + 1) * LANES]
+        for xo in range(BOX_X // SUBLANES):
+            shifted = 0.5 * (potential_ref[xo * SUBLANES:(xo + 1) * SUBLANES, yo * LANES:(yo + 1) * LANES] - 1.0)
+            for fun in range(FUN_DEV):
+                start = xo * SUBLANES * x_rows + yo * FUN_DEV + fun
+                plane_ref[pl.ds(start, SUBLANES, stride=x_rows), :] = shifted
+
+    def rows_of(far, xi, out):
+        return pl.ds((far * 32 + out * X_IN + xi) * x_rows, x_rows)
+
+    arrivals[1].wait()
     for xi in range(X_IN):
-        for yo in range(Y_OUT):
-            potential = plane_ref[pl.ds(yo * BOX_X + xi, SUBLANES, stride=X_IN), :]
-            shift_ref[xi, yo] = 0.5 * (potential - 1.0)
-
-    def stencil_step(source, target, coefficient, last, first):
-        zero = jnp.zeros((SUBLANES, LANES), jnp.float32)
-        for xi in range(X_IN):
-            line = [source[xi, yo] for yo in range(Y_OUT)]
-            up = [pltpu.roll(v, 96, 1) for v in line] + [zero]
-            down = [zero] + [pltpu.roll(v, 32, 1) for v in line]
-            for yo in range(Y_OUT):
-                v = line[yo]
-                if xi < X_IN - 1:
-                    right = source[xi + 1, yo]
-                else:
-                    right = jnp.where(row < SUBLANES - 1, pltpu.roll(source[0, yo], SUBLANES - 1, 0), 0.0)
-                if xi > 0:
-                    left = source[xi - 1, yo]
-                else:
-                    left = jnp.where(row > 0, pltpu.roll(source[X_IN - 1, yo], 1, 0), 0.0)
-                total = left + right
-                total = total + jnp.where(lane < 96, up[yo], up[yo + 1])
-                total = total + jnp.where(lane >= 32, down[yo + 1], down[yo])
-                total = total + jnp.where(z < 31, pltpu.roll(v, 127, 1), 0.0)
-                total = total + jnp.where(z > 0, pltpu.roll(v, 1, 1), 0.0)
-                applied = shift_ref[xi, yo] * v - 0.25 * total
-                if last:
-                    applied = 0.5 * applied
-                value = coefficient * field_ref[xi, yo] + applied
-                if not first:
-                    value = value - target[xi, yo]
-                target[xi, yo] = value
-
-    def one_function(fun, carry):
-        for xi in range(X_IN):
-            for yo in range(Y_OUT):
-                start = (xi * Y_OUT + yo) * FUN_DEV + fun
-                field_ref[xi, yo] = wide_ref[pl.ds(start, SUBLANES, stride=X_IN * Y_OUT * FUN_DEV), :]
-
-        def one_update(update, carry):
+        blocks = [(far, out) for far in range(X_FAR) for out in range(4)]
+        fields = jnp.concatenate([in_ref[rows_of(far, xi, out), :] for far, out in blocks], 0)
+        fields = lax.dot_general(order_z, fields, (((1,), (1,)), ((), ())), preferred_element_type=jnp.float32)
+        for far in range(X_FAR):
+            field_ref[far, xi] = fields[:, far * LANES:(far + 1) * LANES].reshape(PARTS, SUBLANES, LANES)
+            shifts = jnp.concatenate([plane_ref[rows_of(far, xi, out), :] for out in range(4)], 0)
+            turned_ref[far] = shifts.T
+            for part in range(PARTS):
+                shift_ref[far, xi, part] = turned_ref[far, pl.ds(part // 4 * 32 + part % 4, SUBLANES, stride=4), :]
+
+    def plane_step(before, at, after, target, coefficient, scale, last, start, far, xi):
+        for part in range(PARTS):
+            yi, zi = part // 4, part % 4
+            total = before[part] + after[part]
+            if zi < 3:
+                total = total + at[part + 1]
+            else:
+                total = total + jnp.where(row < SUBLANES - 1, pltpu.roll(at[yi * 4], SUBLANES - 1, 0), 0.0)
+            if zi > 0:
+                total = total + at[part - 1]
+            else:
+                total = total + jnp.where(row > 0, pltpu.roll(at[yi * 4 + 3], 1, 0), 0.0)
+            if yi < 3:
+                total = total + at[part + 4]
+            else:
+                total = total + jnp.where(y_out < Y_OUT - 1, pltpu.roll(at[zi], LANES - FUN_DEV, 1), 0.0)
+            if yi > 0:
+                total = total + at[part - 4]
+            else:
+                total = total + jnp.where(y_out > 0, pltpu.roll(at[12 + zi], FUN_DEV, 1), 0.0)
+            applied = shift_ref[far, xi, part] * at[part] - 0.25 * total
+            if scale is not None:
+                applied = scale * applied
+            value = coefficient * field_ref[far, xi, part] + applied
+            if not start:
+                value = value - target[far, xi, part]
+            if last:
+                field_ref[far, xi, part] = value
+            else:
+                target[far, xi, part] = value
+
+    def stencil_step(source, target, coefficient, scale=None, last=False, start=False):
+        def plane(far, xi):
+            return [source[far, xi, part] for part in range(PARTS)]
+
+        def below(far):
+            own = [pltpu.roll(v, 32, 1) for v in plane(far, X_IN - 1)]
+            if far == 0:
+                return [jnp.where(lane < 32, 0.0, v) for v in own]
+            return [jnp.where(lane < 32, pltpu.roll(v, 32, 1), w) for v, w in zip(plane(0, X_IN - 1), own)]
+
+        def above(far):
+            own = [pltpu.roll(v, 96, 1) for v in plane(far, 0)]
+            if far == 1:
+                return [jnp.where(lane >= 96, 0.0, v) for v in own]
+            return [jnp.where(lane >= 96, pltpu.roll(v, 96, 1), w) for v, w in zip(plane(1, 0), own)]
+
+        for far in range(X_FAR):
+            before, at = below(far), plane(far, 0)
             for xi in range(X_IN):
-                for yo in range(Y_OUT):
-                    even_ref[xi, yo] = coef_ref[DEGREE] * field_ref[xi, yo]
-            source, target = even_ref, odd_ref
-            for order in range(DEGREE - 1, -1, -1):
-                stencil_step(source, target, coef_ref[order], order == 0, order == DEGREE - 1)
-                source, target = target, source
-            for xi in range(X_IN):
-                for yo in range(Y_OUT):
-                    field_ref[xi, yo] = source[xi, yo]
+                after = plane(far, xi + 1) if xi < X_IN - 1 else above(far)
+                plane_step(before, at, after, target, coefficient, scale, last, start, far, xi)
+                before, at = at, after
+
+    def one_update(update, carry):
+        stencil_step(field_ref, odd_ref, coef_ref[DEGREE - 1], scale=coef_ref[DEGREE], start=True)
+        stencil_step(odd_ref, even_ref, coef_ref[DEGREE - 2] - coef_ref[DEGREE], start=True)
+
+        def two_orders(pair, carry):
+            order = DEGREE - 3 - 2 * pair
+            stencil_step(even_ref, odd_ref, coef_ref[order])
+            stencil_step(odd_ref, even_ref, coef_ref[order - 1])
             return carry
 
-        lax.fori_loop(0, UPDATES, one_update, 0)
-        for xi in range(X_IN):
-            for yo in range(Y_OUT):
-                start = (xi * Y_OUT + yo) * FUN_DEV + fun
-                wide_ref[pl.ds(start, SUBLANES, stride=X_IN * Y_OUT * FUN_DEV), :] = field_ref[xi, yo]
+        lax.fori_loop(0, DEGREE // 2 - 2, two_orders, 0)
+        stencil_step(even_ref, odd_ref, coef_ref[1])
+        stencil_step(odd_ref, even_ref, coef_ref[0], scale=0.5, last=True)
         return carry
 
-    lax.fori_loop(0, FUN_DEV, one_function, 0)
-    out_ref[...] = wide_ref[...].astype(jnp.bfloat16)
+    arrivals[2].wait()
+    lax.fori_loop(0, UPDATES, one_update, 0)
+
+    for xi in range(X_IN):
+        fields = field_ref[:, xi].reshape(X_FAR * LANES, LANES).astype(jnp.bfloat16)
+        fields = lax.dot_general(unit, fields, (((1,), (1,)), ((), ())), preferred_element_type=jnp.float32)
+        fields = fields.astype(jnp.bfloat16)
+        for far in range(X_FAR):
+            for out in range(4):
+                rows = fields[out * x_rows:(out + 1) * x_rows, far * LANES:(far + 1) * LANES]
+                out_ref[rows_of(far, xi, out), :] = rows
 
 
 def filter_twice(rows, potential, coefficient):
-    vectors = pltpu.VMEM((X_IN, Y_OUT, SUBLANES, LANES), jnp.float32)
+    vectors = pltpu.VMEM((X_FAR, X_IN, PARTS, SUBLANES, LANES), jnp.float32)
     return pl.pallas_call(
         filter_kernel,
         name="filter_twice",
         out_shape=jax.ShapeDtypeStruct(rows.shape, jnp.bfloat16),
-        in_specs=[
-            pl.BlockSpec(memory_space=pltpu.SMEM),
-            pl.BlockSpec(memory_space=pltpu.VMEM),
-            pl.BlockSpec(memory_space=pltpu.VMEM),
+        in_specs=[pl.BlockSpec(memory_space=pltpu.HBM)] * 3,
+        out_specs=pl.BlockSpec(memory_space=pltpu.VMEM),
+        scratch_shapes=[
+            pltpu.SMEM(coefficient.shape, jnp.float32),
+            pltpu.VMEM(potential.shape, jnp.float32),
+            pltpu.VMEM(rows.shape, jnp.bfloat16),
+            pltpu.VMEM(rows.shape, jnp.float32),
+            pltpu.VMEM((X_FAR, LANES, LANES), jnp.float32),
+            vectors,
+            vectors,
+            vectors,
+            vectors,
+            pltpu.SemaphoreType.DMA((3,)),
         ],
-        out_specs=pl.BlockSpec(memory_space=pltpu.VMEM),
-        scratch_shapes=[pltpu.VMEM(rows.shape, jnp.float32), pltpu.VMEM((BOX_X * Y_OUT, LANES), jnp.float32), vectors, vectors, vectors, vectors],
-        compiler_params=pltpu.CompilerParams(vmem_limit_bytes=16 * 2**20),
+        compiler_params=pltpu.CompilerParams(vmem_limit_bytes=60 * 2**20),
         cost_estimate=pl.CostEstimate(flops=60_000_000, bytes_accessed=40_000_000, transcendentals=0),
     )(coefficient, potential, rows)
 
 
 def mix_kernel(mixer_ref, points_ref, out_ref, middle_ref):
+    points = jnp.dot(points_ref[...], point_order(points_ref.shape[1]), preferred_element_type=jnp.float32)
     middle_ref[...] = jnp.dot(
-        mixer_ref[...], points_ref[...], preferred_element_type=jnp.float32
+        mixer_ref[...], points.astype(jnp.bfloat16), preferred_element_type=jnp.float32
     ).astype(jnp.bfloat16)
     out_ref[...] = jnp.dot(
         mixer_ref[...], middle_ref[...], preferred_element_type=jnp.float32

time: 90.5 us -> 79.9 us (0.88)
  Pallas kernels: 31.4 us -> 21.5 us
  local copies, waits for them, and re-layouts: 4.99 us -> 2.34 us
  starting transfers between devices: 16.2 us -> 17.8 us
    pallas_call x1, Pallas kernels: 20.8 us -> 10.7 us  [filter_twice(): pl.pallas_call(filter_kernel, name='filter_twice', out_shape=jax.ShapeDty...]
    unnamed x15 -> x9, local copies, waits for them, and re-layouts: 4.58 us -> 1.93 us
    all_to_all x1, starting transfers between devices: 14.1 us -> 15.7 us  [local(): lax.all_to_all(outgoing, ('narrow', 'wide'), split_axis=0, concat_axis=0,...]
  transfers between devices with their start and end apart: 2 -> 2, of which waited for: 1 -> 2; matrix products, arithmetic and copies ran while one was open for 0% -> 0% of each run, Pallas kernels for 32% -> 24%
where the time goes in v2:
time: 79.9 us; the launch traced here: 79.7 us
  blocking collectives  26.9 us (34%)
  Pallas kernels  21.5 us (27%)
  starting transfers between devices  17.8 us (22%)
  waiting for transfers between devices  11 us (14%)
  local copies, waits for them, and re-layouts  2.34 us (3%)
    all_to_all x1, blocking collectives, local(): lax.all_to_all(mixed.reshape(devices, FUN_DEV, own), ('narrow', 'wide'),...  26.9 us
    all_to_all x1, starting transfers between devices, local(): lax.all_to_all(outgoing, ('narrow', 'wide'), split_axis=0, concat_axis=0,...  15.7 us
    pallas_call x1, Pallas kernels, filter_twice(): pl.pallas_call(filter_kernel, name='filter_twice', out_shape=jax.ShapeDty...  10.7 us
    all_to_all x1, waiting for transfers between devices, local(): lax.all_to_all(outgoing, ('narrow', 'wide'), split_axis=0, concat_axis=0,...  10.5 us
    pallas_call x1, Pallas kernels, dense_mixer(): pl.pallas_call(spread_kernel, name='spread_blocks', out_shape=jax.ShapeDt...  8.41 us
    pallas_call x1, Pallas kernels, mix_twice(): pl.pallas_call(mix_kernel, name='mix_twice', out_shape=jax.ShapeDtypeStru...  2.44 us
    ppermute x1, starting transfers between devices, local(): lax.ppermute(kernel_halves, ('wide', 'narrow'), other_half_pairs(lax.axis...  2.13 us
    unnamed x9, local copies, waits for them, and re-layouts  1.93 us
  transfers between devices with their start and end apart: 2, of which 2 were waited for; matrix products, arithmetic and copies ran while one was open for 0% of the time, Pallas kernels for 24%

profile of v2, /device:TPU:1, one launch (start us, length us, event | category | flops | bytes accessed | tf_op | source)
XLA Modules:
  0.0 79.7 jit_solution(4124406229927367534)
XLA Ops:
  0.0 0.0 copy-start
  0.0 0.0 copy-start.3
  0.0 2.1 %collective-permute-start = (bf16[1,16,12,2048]{3,1,2,0:T(8,128)(2,1)}, bf16[1,16,12,2048]{3,1,2,0:T(8,128)(2,1)S(1)}, u32[]{:S(2)}, u32[]{:S(2)}) collective-permute-start(bf16[1,16,12,2048]{3,1,2,0:T(8,128)(2,1)} %param.9), channel_id=1, source_target_pairs={{1,0},{32,1},{35,2},{2,3},{5,4},{36,5},{39,6},{6,7},{9,8},{40,9},{... | collective-permute-start | bytes 2359304 | tf_op jit(solution)/shard_map/ppermute | solution.py:305
  2.1 10.7 %filter_twice.1 = bf16[2048,128]{1,0:T(8,128)(2,1)} custom-call(f32[9]{0:T(128)} %coef_hbm.1, f32[64,1024]{1,0:T(8,128)} %potential_hbm.1, bf16[2048,128]{1,0:T(8,128)(2,1)} %bitcast.29), custom_call_target="tpu_custom_call" | custom-call | flops 60000000 | bytes 40000000 | tf_op jit(solution)/shard_map/filter_twice/pallas_call | solution.py:187
  12.8 0.4 collective-permute-done
  13.2 0.0 copy-start.1
  13.2 15.7 %all-to-all-start = ((bf16[256,4,256]{2,1,0:T(4,128)(2,1)}), bf16[256,4,256]{2,1,0:T(4,128)(2,1)S(1)}, u32[]{:S(2)}, u32[]{:S(2)}) async-start(bf16[256,4,256]{2,1,0:T(4,128)(2,1)} %bitcast.27), calls=%async_computation | async-start | bytes 1048576 | tf_op jit(solution)/shard_map/all_to_all | solution.py:314
  28.9 0.0 copy-done.3
  28.9 0.1 copy.8
  29.0 0.1 eq.32
  29.1 0.1 and_convert_fusion.place_ref
  29.2 0.0 copy-done.1
  29.2 0.0 copy-done
  29.3 0.0 copy-start.2
  29.3 1.1 %copy-done.2 = bf16[1,16,12,2048]{3,1,2,0:T(8,128)(2,1)S(1)} copy-done((bf16[1,16,12,2048]{3,1,2,0:T(8,128)(2,1)S(1)}, bf16[1,16,12,2048]{3,1,2,0:T(8,128)(2,1)}, u32[]{:S(2)}) %copy-start.2) | copy-done | bytes 786456
  30.4 8.4 %spread_blocks.1.mixer_ref = bf16[1024,1024]{1,0:T(8,128)(2,1)S(1)} custom-call(s32[1]{0:T(128)} %bitcast.half_ref, bf16[256,192]{1,0:T(8,128)(2,1)S(1)} %and_convert_fusion.place_ref, bf16[192,2048]{1,0:T(8,128)(2,1)S(1)} %bitcast.25, bf16[192,2048]{1,0:T(8,128)(2,1)S(1)} %bitcast.26), custom_call_target="tpu_custom_call" | custom-call | flops 400000000 | bytes 15000000 | tf_op jit(solution)/shard_map/spread_blocks/pallas_call | solution.py:278
  38.8 10.5 %all-to-all-done = bf16[256,4,256]{2,1,0:T(4,128)(2,1)S(1)} async-done(((bf16[256,4,256]{2,1,0:T(4,128)(2,1)}), bf16[256,4,256]{2,1,0:T(4,128)(2,1)S(1)}, u32[]{:S(2)}, u32[]{:S(2)}) %all-to-all-start) | async-done | bytes 524320 | tf_op jit(solution)/shard_map/all_to_all | solution.py:314
  49.3 0.1 reshape.105.points_ref
  49.5 2.4 %mix_twice.1 = bf16[1024,256]{1,0:T(8,128)(2,1)S(1)} custom-call(bf16[1024,1024]{1,0:T(8,128)(2,1)S(1)} %spread_blocks.1.mixer_ref, bf16[1024,256]{1,0:T(8,128)(2,1)S(1)} %reshape.105.points_ref), custom_call_target="tpu_custom_call" | custom-call | flops 1100000000 | bytes 4000000 | tf_op jit(solution)/shard_map/mix_twice/pallas_call | solution.py:221
  51.9 0.1 reshape.106
  52.1 26.9 %all_to_all.10 = bf16[256,4,256]{2,1,0:T(4,128)(2,1)S(1)} all-to-all(bf16[256,4,256]{2,1,0:T(4,128)(2,1)S(1)} %reshape.106), channel_id=1, replica_groups=mesh['wide'=128,'narrow'=2] {'narrow','wide'}, dimensions={0} | all-to-all | bytes 1048576 | tf_op jit(solution)/shard_map/all_to_all | solution.py:316
  78.9 0.8 copy.12
  (2 shorter events, 0.0 us)
Async XLA Ops:
  0.0 29.3 %copy-start = (bf16[1,16,12,2048]{3,1,2,0:T(8,128)(2,1)S(1)}, bf16[1,16,12,2048]{3,1,2,0:T(8,128)(2,1)}, u32[]{:S(2)}) copy-start(bf16[1,16,12,2048]{3,1,2,0:T(8,128)(2,1)} %param.9) | copy-start | bytes 2359300
  0.0 28.9 %copy-start.3 = (s32[16,12]{1,0:T(8,128)S(1)}, s32[16,12]{1,0:T(8,128)}, u32[]{:S(2)}) copy-start(s32[16,12]{1,0:T(8,128)} %param.8) | copy-start | bytes 2308
  0.0 13.2 %collective-permute-start = (bf16[1,16,12,2048]{3,1,2,0:T(8,128)(2,1)}, bf16[1,16,12,2048]{3,1,2,0:T(8,128)(2,1)S(1)}, u32[]{:S(2)}, u32[]{:S(2)}) collective-permute-start(bf16[1,16,12,2048]{3,1,2,0:T(8,128)(2,1)} %param.9), channel_id=1, source_target_pairs={{1,0},{32,1},{35,2},{2,3},{5,4},{36,5},{39,6},{6,7},{9,8},{40,9},{... | collective-permute-start | bytes 2359304 | tf_op jit(solution)/shard_map/ppermute | solution.py:305
  13.2 16.0 %copy-start.1 = (bf16[1,16,12,2048]{3,1,2,0:T(8,128)(2,1)}, bf16[1,16,12,2048]{3,1,2,0:T(8,128)(2,1)S(1)}, u32[]{:S(2)}) copy-start(bf16[1,16,12,2048]{3,1,2,0:T(8,128)(2,1)S(1)} %collective-permute-done) | copy-start | bytes 2359300
  13.2 36.1 %all-to-all-start = ((bf16[256,4,256]{2,1,0:T(4,128)(2,1)}), bf16[256,4,256]{2,1,0:T(4,128)(2,1)S(1)}, u32[]{:S(2)}, u32[]{:S(2)}) async-start(bf16[256,4,256]{2,1,0:T(4,128)(2,1)} %bitcast.27), calls=%async_computation | async-start | bytes 1048576 | tf_op jit(solution)/shard_map/all_to_all | solution.py:314
  29.3 1.1 %copy-start.2 = (bf16[1,16,12,2048]{3,1,2,0:T(8,128)(2,1)S(1)}, bf16[1,16,12,2048]{3,1,2,0:T(8,128)(2,1)}, u32[]{:S(2)}) copy-start(bf16[1,16,12,2048]{3,1,2,0:T(8,128)(2,1)} %copy-done.1) | copy-start | bytes 2359300

commit v3 on v2

--- a/solution.py
+++ b/solution.py
@@ -208,13 +208,15 @@
 
 
 def mix_kernel(mixer_ref, points_ref, out_ref, middle_ref):
-    points = jnp.dot(points_ref[...], point_order(points_ref.shape[1]), preferred_element_type=jnp.float32)
-    middle_ref[...] = jnp.dot(
-        mixer_ref[...], points.astype(jnp.bfloat16), preferred_element_type=jnp.float32
-    ).astype(jnp.bfloat16)
-    out_ref[...] = jnp.dot(
-        mixer_ref[...], middle_ref[...], preferred_element_type=jnp.float32
-    ).astype(jnp.bfloat16)
+    size = points_ref.shape[1]
+    points = jnp.dot(points_ref[...], point_order(size), preferred_element_type=jnp.float32).astype(jnp.bfloat16)
+    for start in range(0, FUNCS, size):
+        part = jnp.dot(mixer_ref[start:start + size, :], points, preferred_element_type=jnp.float32)
+        middle_ref[start:start + size, :] = part.astype(jnp.bfloat16)
+    points = middle_ref[...]
+    for start in range(0, FUNCS, size):
+        part = jnp.dot(mixer_ref[start:start + size, :], points, preferred_element_type=jnp.float32)
+        out_ref[start:start + size, :] = part.astype(jnp.bfloat16)
 
 
 def mix_twice(mixer, points):
@@ -230,17 +232,22 @@
     )(mixer, points)
 
 
-def spread_kernel(half_ref, place_ref, own_ref, other_ref, out_ref, wide_ref):
+def spread_kernel(half_ref, place_ref, swapped_ref, own_ref, near_ref, far_ref, out_ref, wide_ref):
     lane = lax.broadcasted_iota(jnp.int32, (SUBLANES, LANES), 1)
     row_blocks = FUNCS // BLOCK
     column_tiles = FUNCS // 2 // LANES
-    for source_ref, half in ((own_ref, half_ref[0]), (other_ref, 1 - half_ref[0])):
-        def one_pair(pair, carry, source_ref=source_ref, half=half):
-            spread = jnp.dot(
-                place_ref[...],
-                source_ref[:, pl.ds(pl.multiple_of(pair * 2 * LANES, 2 * LANES), 2 * LANES)],
-                preferred_element_type=jnp.float32,
-            )
+    sides = (
+        (place_ref, (own_ref,), half_ref[0]),
+        (swapped_ref, (near_ref, far_ref), 1 - half_ref[0]),
+    )
+
+    def one_pair(pair, carry):
+        columns = pl.ds(pl.multiple_of(pair * 2 * LANES, 2 * LANES), 2 * LANES)
+        spreads = []
+        for where_ref, source_refs, _ in sides:
+            entries = jnp.concatenate([source_ref[:, columns] for source_ref in source_refs], 0)
+            spreads.append(jnp.dot(where_ref[...], entries, preferred_element_type=jnp.float32))
+        for spread, (_, _, half) in zip(spreads, sides):
             for side in range(2):
                 for tile in range(column_tiles):
                     for rows in range(row_blocks // SUBLANES):
@@ -256,35 +263,40 @@
                             start = (half * column_tiles + tile) * FUNCS
                             start = start + side * (FUNCS // 2) + rows * SUBLANES * (BLOCK // 2) + pair * FUN_DEV + fun
                             wide_ref[pl.ds(start, SUBLANES, stride=BLOCK // 2), :] = value
-            return carry
-
-        lax.fori_loop(0, BLOCK * BLOCK // 2 // (2 * LANES), one_pair, 0)
+        return carry
+
+    lax.fori_loop(0, BLOCK * BLOCK // 2 // (2 * LANES), one_pair, 0)
     for tile in range(FUNCS // LANES):
         out_ref[:, tile * LANES:(tile + 1) * LANES] = wide_ref[tile * FUNCS:(tile + 1) * FUNCS, :].astype(jnp.bfloat16)
 
 
-def dense_mixer(half, own, other, block_cols):
+def dense_mixer(half, core, own, near, far, block_cols):
     row_blocks, slots = block_cols.shape
     entry = jnp.arange(slots * row_blocks)
     place = jnp.arange(row_blocks * row_blocks)
     column = block_cols.T.reshape(-1)
-    chosen = (column[None, :] == place[:, None] // row_blocks) & (
-        entry[None, :] % row_blocks == place[:, None] % row_blocks
-    )
+    cut = column.shape[0] // 2
+    swapped = jnp.where(core == 0, column, jnp.concatenate([column[cut:], column[:cut]]))
+
+    def chosen(column):
+        return (
+            (column[None, :] == place[:, None] // row_blocks)
+            & (entry[None, :] % row_blocks == place[:, None] % row_blocks)
+        ).astype(jnp.bfloat16)
 
     def flat(blocks):
-        return blocks[0].transpose(1, 0, 2).reshape(slots * row_blocks, BLOCK * BLOCK // 2)
+        return blocks[0].transpose(1, 0, 2).reshape(-1, BLOCK * BLOCK // 2)
 
     return pl.pallas_call(
         spread_kernel,
         name="spread_blocks",
         out_shape=jax.ShapeDtypeStruct((FUNCS, FUNCS), jnp.bfloat16),
-        in_specs=[pl.BlockSpec(memory_space=pltpu.SMEM)] + [pl.BlockSpec(memory_space=pltpu.VMEM)] * 3,
+        in_specs=[pl.BlockSpec(memory_space=pltpu.SMEM)] + [pl.BlockSpec(memory_space=pltpu.VMEM)] * 5,
         out_specs=pl.BlockSpec(memory_space=pltpu.VMEM),
         scratch_shapes=[pltpu.VMEM((FUNCS * FUNCS // LANES, LANES), jnp.float32)],
-        compiler_params=pltpu.CompilerParams(vmem_limit_bytes=16 * 2**20),
+        compiler_params=pltpu.CompilerParams(vmem_limit_bytes=60 * 2**20),
         cost_estimate=pl.CostEstimate(flops=400_000_000, bytes_accessed=15_000_000, transcendentals=0),
-    )(half.reshape(1), chosen.astype(jnp.bfloat16), flat(own), flat(other))
+    )(half.reshape(1), chosen(column), chosen(swapped), flat(own), flat(near), flat(far))
 
 
 def other_half_pairs(wide, narrow):
@@ -302,13 +314,16 @@
 def local(functions, potential, cheb_coef, block_cols, kernel_halves):
     devices = lax.axis_size("wide") * lax.axis_size("narrow")
     own = GRID // devices
-    other = lax.ppermute(
-        kernel_halves, ("wide", "narrow"), other_half_pairs(lax.axis_size("wide"), lax.axis_size("narrow"))
-    )
+    wide, narrow = lax.axis_size("wide"), lax.axis_size("narrow")
+    core = lax.axis_index("wide") % 2
+    slots = kernel_halves.shape[2] // 2
+    part = lax.dynamic_slice_in_dim(kernel_halves, core * slots, slots, 2)
+    near = lax.ppermute(part, ("wide", "narrow"), other_half_pairs(wide, narrow))
     rows = functions.reshape(FUN_DEV, TILES, LANES).transpose(1, 0, 2).reshape(TILES * FUN_DEV, LANES)
     filtered = filter_twice(rows, potential, cheb_coef)
-    filtered, other = lax.optimization_barrier((filtered, other))
-    mixer = dense_mixer(lax.axis_index("narrow"), kernel_halves, other, block_cols)
+    filtered, near = lax.optimization_barrier((filtered, near))
+    far = lax.ppermute(near, "wide", [(index, index ^ 1) for index in range(wide)])
+    mixer = dense_mixer(lax.axis_index("narrow"), core, kernel_halves, near, far, block_cols)
     outgoing = filtered.reshape(devices, own // LANES, FUN_DEV, LANES).transpose(0, 2, 1, 3)
     outgoing = outgoing.reshape(devices, FUN_DEV, own)
     points = lax.all_to_all(outgoing, ("narrow", "wide"), split_axis=0, concat_axis=0, tiled=True)

time: 79.9 us -> 79.7 us (level)
  waiting for transfers between devices: 11 us -> 6.8 us
  local copies, waits for them, and re-layouts: 2.34 us -> 4.98 us
  other arithmetic: 0.15 us -> 0.96 us
    all_to_all x1, waiting for transfers between devices: 10.5 us -> 6.33 us  [local(): lax.all_to_all(outgoing, ('narrow', 'wide'), split_axis=0, concat_axis=0,...]
    ppermute x1 -> x2, starting transfers between devices: 2.13 us -> 4.38 us  [the longest x1 2.2 us: local(): lax.ppermute(part, ('wide', 'narrow'), other_half_pairs(wide, narrow))]
    all_to_all x1, starting transfers between devices: 15.7 us -> 14.1 us  [local(): lax.all_to_all(outgoing, ('narrow', 'wide'), split_axis=0, concat_axis=0,...]
    unnamed x9, local copies, waits for them, and re-layouts: 1.93 us -> 3.13 us
    dynamic_slice x0 -> x1, local copies, waits for them, and re-layouts: none -> 1.03 us  [local(): part = lax.dynamic_slice_in_dim(kernel_halves, core * slots, slots, 2)]
    pallas_call x1, Pallas kernels: 2.44 us -> 1.47 us  [mix_twice(): pl.pallas_call(mix_kernel, name='mix_twice', out_shape=jax.ShapeDtypeStru...]
  transfers between devices with their start and end apart: 2 -> 3, of which waited for: 2 -> 2; matrix products, arithmetic and copies ran while one was open for 0% -> 2% of each run, Pallas kernels for 24% -> 25%
where the time goes in v3:
time: 79.7 us; the launch traced here: 79.5 us
  blocking collectives  26.9 us (34%)
  Pallas kernels  21.3 us (27%)
  starting transfers between devices  18.5 us (23%)
  waiting for transfers between devices  6.8 us (9%)
  local copies, waits for them, and re-layouts  4.98 us (6%)
  other arithmetic  0.96 us (1%)
    all_to_all x1, blocking collectives, local(): lax.all_to_all(mixed.reshape(devices, FUN_DEV, own), ('narrow', 'wide'),...  26.9 us
    all_to_all x1, starting transfers between devices, local(): lax.all_to_all(outgoing, ('narrow', 'wide'), split_axis=0, concat_axis=0,...  14.1 us
    pallas_call x1, Pallas kernels, filter_twice(): pl.pallas_call(filter_kernel, name='filter_twice', out_shape=jax.ShapeDty...  10.7 us
    pallas_call x1, Pallas kernels, dense_mixer(): pl.pallas_call(spread_kernel, name='spread_blocks', out_shape=jax.ShapeDt...  9.18 us
    all_to_all x1, waiting for transfers between devices, local(): lax.all_to_all(outgoing, ('narrow', 'wide'), split_axis=0, concat_axis=0,...  6.33 us
    unnamed x9, local copies, waits for them, and re-layouts  3.13 us
    ppermute x1, starting transfers between devices, local(): lax.ppermute(part, ('wide', 'narrow'), other_half_pairs(wide, narrow))  2.2 us
    ppermute x1, starting transfers between devices, local(): lax.ppermute(near, 'wide', [(index, index ^ 1) for index in range(wide)])  2.17 us
  transfers between devices with their start and end apart: 3, of which 2 were waited for; matrix products, arithmetic and copies ran while one was open for 2% of the time, Pallas kernels for 25%

profile of v3, /device:TPU:1, one launch (start us, length us, event | category | flops | bytes accessed | tf_op | source)
XLA Modules:
  0.0 79.5 jit_solution(4879419354009648070)
XLA Ops:
  0.0 0.0 copy-start.3
  0.0 1.0 %constant_dynamic-slice_fusion = bf16[1,16,6,2048]{3,1,2,0:T(8,128)(2,1)S(1)} fusion(bf16[1,16,12,2048]{3,1,2,0:T(8,128)(2,1)} %param.9, s32[]{:T(128)S(6)} %select_n.71), kind=kLoop, calls=%fused_computation.13 | loop fusion | bytes 786436 | tf_op jit(solution)/shard_map/dynamic_slice | solution.py:320
  1.0 2.2 %collective-permute-start = (bf16[1,16,6,2048]{3,1,2,0:T(8,128)(2,1)S(1)}, bf16[1,16,6,2048]{3,1,2,0:T(8,128)(2,1)S(1)}, u32[]{:S(2)}, u32[]{:S(2)}) collective-permute-start(bf16[1,16,6,2048]{3,1,2,0:T(8,128)(2,1)S(1)} %constant_dynamic-slice_fusion), channel_id=1, source_target_pairs={{1,0},{32,1},{35,2},{2,3},{5,4},{36,5},{39,6},{6,7},{9,8},{40,9},{... | collective-permute-start | bytes 1179656 | tf_op jit(solution)/shard_map/ppermute | solution.py:321
  3.2 10.7 %filter_twice.1 = bf16[2048,128]{1,0:T(8,128)(2,1)} custom-call(f32[9]{0:T(128)} %coef_hbm.1, f32[64,1024]{1,0:T(8,128)} %potential_hbm.1, bf16[2048,128]{1,0:T(8,128)(2,1)} %bitcast.33), custom_call_target="tpu_custom_call" | custom-call | flops 60000000 | bytes 40000000 | tf_op jit(solution)/shard_map/filter_twice/pallas_call | solution.py:187
  13.9 0.0 collective-permute-done
  13.9 0.0 copy-start.1
  13.9 14.1 %all-to-all-start = ((bf16[256,4,256]{2,1,0:T(4,128)(2,1)}), bf16[256,4,256]{2,1,0:T(4,128)(2,1)S(1)}, u32[]{:S(2)}, u32[]{:S(2)}) async-start(bf16[256,4,256]{2,1,0:T(4,128)(2,1)} %bitcast.30), calls=%async_computation | async-start | bytes 1048576 | tf_op jit(solution)/shard_map/all_to_all | solution.py:329
  28.1 0.0 copy-done.3
  28.1 0.1 copy.10
  28.1 0.1 eq.65
  28.2 0.1 fusion.4
  28.3 0.1 copy.11
  28.4 0.1 concatenate.11
  28.5 0.1 copy.12
  28.5 0.1 concatenate.12
  28.6 0.1 add_select_fusion
  28.7 2.2 %collective-permute-start.1 = (bf16[1,16,6,2048]{3,1,2,0:T(8,128)(2,1)S(1)}, bf16[1,16,6,2048]{3,1,2,0:T(8,128)(2,1)S(1)}, u32[]{:S(2)}, u32[]{:S(2)}) collective-permute-start(bf16[1,16,6,2048]{3,1,2,0:T(8,128)(2,1)S(1)} %collective-permute-done), channel_id=1, source_target_pairs={{0,2},{2,0},{4,6},{6,4},{8,10},{10,8},{12,14},{14,12},{16,18},{18,... | collective-permute-start | bytes 1179656 | tf_op jit(solution)/shard_map/ppermute | solution.py:325
  30.9 0.9 %fusion.1 = (bf16[256,192]{1,0:T(8,128)(2,1)}, bf16[256,192]{1,0:T(8,128)(2,1)}) fusion(s32[192]{0:T(256)S(1)} %add_select_fusion, s32[192]{0:T(256)S(1)} %and_select_fusion.1, s32[256]{0:T(256)S(1)} %get-tuple-element.13, s32[256]{0:T(256)S(1)} %get-tuple-element.14, s32[192]{0:T(256)S(1)} %eq.65), kind=kLoop, calls=%fused_computation.3 | loop fusion | flops 344064 | bytes 200960 | tf_op jit(solution)/shard_map/convert_element_type | solution.py:285
  31.8 0.5 collective-permute-done.1
  32.2 0.0 copy-start.2
  32.2 0.0 copy-done.1
  32.2 0.7 copy-done.2
  33.0 9.2 %spread_blocks.1.mixer_ref = bf16[1024,1024]{1,0:T(8,128)(2,1)} custom-call(s32[1]{0:T(128)} %bitcast.half_ref, bf16[256,192]{1,0:T(8,128)(2,1)} %get-tuple-element.12.place_ref, bf16[256,192]{1,0:T(8,128)(2,1)} %get-tuple-element.11.swapped_ref, bf16[192,2048]{1,0:T(8,128)(2,1)} %bitcast.32, bf16[96,2048]{1,0:T(8,128)(2,1)} %bitcast.34, ...), custom_call_target="tpu_custom_call" | custom-call | flops 400000000 | bytes 15000000 | tf_op jit(solution)/shard_map/spread_blocks/pallas_call | solution.py:290
  42.2 6.3 %all-to-all-done = bf16[256,4,256]{2,1,0:T(4,128)(2,1)S(1)} async-done(((bf16[256,4,256]{2,1,0:T(4,128)(2,1)}), bf16[256,4,256]{2,1,0:T(4,128)(2,1)S(1)}, u32[]{:S(2)}, u32[]{:S(2)}) %all-to-all-start) | async-done | bytes 524320 | tf_op jit(solution)/shard_map/all_to_all | solution.py:329
  48.5 0.1 reshape.133.points_ref
  48.6 0.0 copy-start
  48.6 1.6 %copy-done = bf16[1024,1024]{1,0:T(8,128)(2,1)S(1)} copy-done((bf16[1024,1024]{1,0:T(8,128)(2,1)S(1)}, bf16[1024,1024]{1,0:T(8,128)(2,1)}, u32[]{:S(2)}) %copy-start) | copy-done | bytes 2097176
  50.2 1.5 %mix_twice.1 = bf16[1024,256]{1,0:T(8,128)(2,1)S(1)} custom-call(bf16[1024,1024]{1,0:T(8,128)(2,1)S(1)} %copy-done, bf16[1024,256]{1,0:T(8,128)(2,1)S(1)} %reshape.133.points_ref), custom_call_target="tpu_custom_call" | custom-call | flops 1100000000 | bytes 4000000 | tf_op jit(solution)/shard_map/mix_twice/pallas_call | solution.py:223
  51.7 0.1 reshape.134
  51.8 26.9 %all_to_all.10 = bf16[256,4,256]{2,1,0:T(4,128)(2,1)S(1)} all-to-all(bf16[256,4,256]{2,1,0:T(4,128)(2,1)S(1)} %reshape.134), channel_id=1, replica_groups=mesh['wide'=128,'narrow'=2] {'narrow','wide'}, dimensions={0} | all-to-all | bytes 1048576 | tf_op jit(solution)/shard_map/all_to_all | solution.py:331
  78.7 0.8 copy.16
  (2 shorter events, 0.0 us)
Async XLA Ops:
  0.0 28.1 %copy-start.3 = (s32[16,12]{1,0:T(8,128)S(1)}, s32[16,12]{1,0:T(8,128)}, u32[]{:S(2)}) copy-start(s32[16,12]{1,0:T(8,128)} %param.8) | copy-start | bytes 2308
  1.0 12.9 %collective-permute-start = (bf16[1,16,6,2048]{3,1,2,0:T(8,128)(2,1)S(1)}, bf16[1,16,6,2048]{3,1,2,0:T(8,128)(2,1)S(1)}, u32[]{:S(2)}, u32[]{:S(2)}) collective-permute-start(bf16[1,16,6,2048]{3,1,2,0:T(8,128)(2,1)S(1)} %constant_dynamic-slice_fusion), channel_id=1, source_target_pairs={{1,0},{32,1},{35,2},{2,3},{5,4},{36,5},{39,6},{6,7},{9,8},{40,9},{... | collective-permute-start | bytes 1179656 | tf_op jit(solution)/shard_map/ppermute | solution.py:321
  13.9 18.3 %copy-start.1 = (bf16[1,16,6,2048]{3,1,2,0:T(8,128)(2,1)}, bf16[1,16,6,2048]{3,1,2,0:T(8,128)(2,1)S(1)}, u32[]{:S(2)}) copy-start(bf16[1,16,6,2048]{3,1,2,0:T(8,128)(2,1)S(1)} %collective-permute-done) | copy-start | bytes 1179652
  13.9 34.6 %all-to-all-start = ((bf16[256,4,256]{2,1,0:T(4,128)(2,1)}), bf16[256,4,256]{2,1,0:T(4,128)(2,1)S(1)}, u32[]{:S(2)}, u32[]{:S(2)}) async-start(bf16[256,4,256]{2,1,0:T(4,128)(2,1)} %bitcast.30), calls=%async_computation | async-start | bytes 1048576 | tf_op jit(solution)/shard_map/all_to_all | solution.py:329
  28.7 3.5 %collective-permute-start.1 = (bf16[1,16,6,2048]{3,1,2,0:T(8,128)(2,1)S(1)}, bf16[1,16,6,2048]{3,1,2,0:T(8,128)(2,1)S(1)}, u32[]{:S(2)}, u32[]{:S(2)}) collective-permute-start(bf16[1,16,6,2048]{3,1,2,0:T(8,128)(2,1)S(1)} %collective-permute-done), channel_id=1, source_target_pairs={{0,2},{2,0},{4,6},{6,4},{8,10},{10,8},{12,14},{14,12},{16,18},{18,... | collective-permute-start | bytes 1179656 | tf_op jit(solution)/shard_map/ppermute | solution.py:325
  32.2 0.8 copy-start.2
  48.6 1.6 %copy-start = (bf16[1024,1024]{1,0:T(8,128)(2,1)S(1)}, bf16[1024,1024]{1,0:T(8,128)(2,1)}, u32[]{:S(2)}) copy-start(bf16[1024,1024]{1,0:T(8,128)(2,1)} %spread_blocks.1.mixer_ref) | copy-start | bytes 6291460

commit v4 on v2

--- a/solution.py
+++ b/solution.py
@@ -101,25 +101,20 @@
                 shift_ref[far, xi, part] = turned_ref[far, pl.ds(part // 4 * 32 + part % 4, SUBLANES, stride=4), :]
 
     def plane_step(before, at, after, target, coefficient, scale, last, start, far, xi):
+        near = {(part // 4, part % 4): at[part] for part in range(PARTS)}
+        for index in range(4):
+            near[index, 4] = jnp.where(row < SUBLANES - 1, pltpu.roll(near[index, 0], SUBLANES - 1, 0), 0.0)
+            near[index, -1] = jnp.where(row > 0, pltpu.roll(near[index, 3], 1, 0), 0.0)
+            near[4, index] = jnp.where(y_out < Y_OUT - 1, pltpu.roll(near[0, index], LANES - FUN_DEV, 1), 0.0)
+            near[-1, index] = jnp.where(y_out > 0, pltpu.roll(near[3, index], FUN_DEV, 1), 0.0)
+        ahead = {}
+        for yi in range(-1, 4):
+            for zi in range(-1, 4):
+                if (yi, zi) not in ((-1, 3), (3, -1)):
+                    ahead[yi, zi] = near[yi, zi + 1] + near[yi + 1, zi]
         for part in range(PARTS):
             yi, zi = part // 4, part % 4
-            total = before[part] + after[part]
-            if zi < 3:
-                total = total + at[part + 1]
-            else:
-                total = total + jnp.where(row < SUBLANES - 1, pltpu.roll(at[yi * 4], SUBLANES - 1, 0), 0.0)
-            if zi > 0:
-                total = total + at[part - 1]
-            else:
-                total = total + jnp.where(row > 0, pltpu.roll(at[yi * 4 + 3], 1, 0), 0.0)
-            if yi < 3:
-                total = total + at[part + 4]
-            else:
-                total = total + jnp.where(y_out < Y_OUT - 1, pltpu.roll(at[zi], LANES - FUN_DEV, 1), 0.0)
-            if yi > 0:
-                total = total + at[part - 4]
-            else:
-                total = total + jnp.where(y_out > 0, pltpu.roll(at[12 + zi], FUN_DEV, 1), 0.0)
+            total = before[part] + after[part] + (ahead[yi, zi] + ahead[yi - 1, zi - 1])
             applied = shift_ref[far, xi, part] * at[part] - 0.25 * total
             if scale is not None:
                 applied = scale * applied
@@ -208,13 +203,15 @@
 
 
 def mix_kernel(mixer_ref, points_ref, out_ref, middle_ref):
-    points = jnp.dot(points_ref[...], point_order(points_ref.shape[1]), preferred_element_type=jnp.float32)
-    middle_ref[...] = jnp.dot(
-        mixer_ref[...], points.astype(jnp.bfloat16), preferred_element_type=jnp.float32
-    ).astype(jnp.bfloat16)
-    out_ref[...] = jnp.dot(
-        mixer_ref[...], middle_ref[...], preferred_element_type=jnp.float32
-    ).astype(jnp.bfloat16)
+    size = points_ref.shape[1]
+    points = jnp.dot(points_ref[...], point_order(size), preferred_element_type=jnp.float32).astype(jnp.bfloat16)
+    for start in range(0, FUNCS, size):
+        part = jnp.dot(mixer_ref[start:start + size, :], points, preferred_element_type=jnp.float32)
+        middle_ref[start:start + size, :] = part.astype(jnp.bfloat16)
+    points = middle_ref[...]
+    for start in range(0, FUNCS, size):
+        part = jnp.dot(mixer_ref[start:start + size, :], points, preferred_element_type=jnp.float32)
+        out_ref[start:start + size, :] = part.astype(jnp.bfloat16)
 
 
 def mix_twice(mixer, points):
@@ -234,13 +231,14 @@
     lane = lax.broadcasted_iota(jnp.int32, (SUBLANES, LANES), 1)
     row_blocks = FUNCS // BLOCK
     column_tiles = FUNCS // 2 // LANES
-    for source_ref, half in ((own_ref, half_ref[0]), (other_ref, 1 - half_ref[0])):
-        def one_pair(pair, carry, source_ref=source_ref, half=half):
-            spread = jnp.dot(
-                place_ref[...],
-                source_ref[:, pl.ds(pl.multiple_of(pair * 2 * LANES, 2 * LANES), 2 * LANES)],
-                preferred_element_type=jnp.float32,
-            )
+    sides = ((own_ref, half_ref[0]), (other_ref, 1 - half_ref[0]))
+
+    def one_pair(pair, carry):
+        columns = pl.ds(pl.multiple_of(pair * 2 * LANES, 2 * LANES), 2 * LANES)
+        spreads = []
+        for source_ref, _ in sides:
+            spreads.append(jnp.dot(place_ref[...], source_ref[:, columns], preferred_element_type=jnp.float32))
+        for spread, (_, half) in zip(spreads, sides):
             for side in range(2):
                 for tile in range(column_tiles):
                     for rows in range(row_blocks // SUBLANES):
@@ -256,9 +254,9 @@
                             start = (half * column_tiles + tile) * FUNCS
                             start = start + side * (FUNCS // 2) + rows * SUBLANES * (BLOCK // 2) + pair * FUN_DEV + fun
                             wide_ref[pl.ds(start, SUBLANES, stride=BLOCK // 2), :] = value
-            return carry
-
-        lax.fori_loop(0, BLOCK * BLOCK // 2 // (2 * LANES), one_pair, 0)
+        return carry
+
+    lax.fori_loop(0, BLOCK * BLOCK // 2 // (2 * LANES), one_pair, 0)
     for tile in range(FUNCS // LANES):
         out_ref[:, tile * LANES:(tile + 1) * LANES] = wide_ref[tile * FUNCS:(tile + 1) * FUNCS, :].astype(jnp.bfloat16)
 

time: 79.9 us -> 79 us (0.989)
  Pallas kernels: 21.5 us -> 18 us
  waiting for transfers between devices: 11 us -> 13.5 us
    pallas_call x1, Pallas kernels: 8.41 us -> 6.34 us  [dense_mixer(): pl.pallas_call(spread_kernel, name='spread_blocks', out_shape=jax.ShapeDt...]
    all_to_all x1, waiting for transfers between devices: 10.5 us -> 12.6 us  [local(): lax.all_to_all(outgoing, ('narrow', 'wide'), split_axis=0, concat_axis=0,...]
    pallas_call x1, Pallas kernels: 2.44 us -> 1.47 us  [mix_twice(): pl.pallas_call(mix_kernel, name='mix_twice', out_shape=jax.ShapeDtypeStru...]
  transfers between devices with their start and end apart: 2 -> 2, of which waited for: 2 -> 2; matrix products, arithmetic and copies ran while one was open for 0% -> 0% of each run, Pallas kernels for 24% -> 21%
where the time goes in v4:
time: 79 us; the launch traced here: 78.8 us
  blocking collectives  26.9 us (34%)
  Pallas kernels  18 us (23%)
  starting transfers between devices  17.8 us (23%)
  waiting for transfers between devices  13.5 us (17%)
  local copies, waits for them, and re-layouts  2.34 us (3%)
    all_to_all x1, blocking collectives, local(): lax.all_to_all(mixed.reshape(devices, FUN_DEV, own), ('narrow', 'wide'),...  26.9 us
    all_to_all x1, starting transfers between devices, local(): lax.all_to_all(outgoing, ('narrow', 'wide'), split_axis=0, concat_axis=0,...  15.7 us
    all_to_all x1, waiting for transfers between devices, local(): lax.all_to_all(outgoing, ('narrow', 'wide'), split_axis=0, concat_axis=0,...  12.6 us
    pallas_call x1, Pallas kernels, filter_twice(): pl.pallas_call(filter_kernel, name='filter_twice', out_shape=jax.ShapeDty...  10.2 us
    pallas_call x1, Pallas kernels, dense_mixer(): pl.pallas_call(spread_kernel, name='spread_blocks', out_shape=jax.ShapeDt...  6.34 us
    ppermute x1, starting transfers between devices, local(): lax.ppermute(kernel_halves, ('wide', 'narrow'), other_half_pairs(lax.axis...  2.13 us
    unnamed x9, local copies, waits for them, and re-layouts  1.93 us
  transfers between devices with their start and end apart: 2, of which 2 were waited for; matrix products, arithmetic and copies ran while one was open for 0% of the time, Pallas kernels for 21%

profile of v4, /device:TPU:1, one launch (start us, length us, event | category | flops | bytes accessed | tf_op | source)
XLA Modules:
  0.0 78.8 jit_solution(6678848669647383841)
XLA Ops:
  0.0 0.0 copy-start
  0.0 0.0 copy-start.3
  0.0 2.1 %collective-permute-start = (bf16[1,16,12,2048]{3,1,2,0:T(8,128)(2,1)}, bf16[1,16,12,2048]{3,1,2,0:T(8,128)(2,1)S(1)}, u32[]{:S(2)}, u32[]{:S(2)}) collective-permute-start(bf16[1,16,12,2048]{3,1,2,0:T(8,128)(2,1)} %param.9), channel_id=1, source_target_pairs={{1,0},{32,1},{35,2},{2,3},{5,4},{36,5},{39,6},{6,7},{9,8},{40,9},{... | collective-permute-start | bytes 2359304 | tf_op jit(solution)/shard_map/ppermute | solution.py:303
  2.1 10.2 %filter_twice.1 = bf16[2048,128]{1,0:T(8,128)(2,1)} custom-call(f32[9]{0:T(128)} %coef_hbm.1, f32[64,1024]{1,0:T(8,128)} %potential_hbm.1, bf16[2048,128]{1,0:T(8,128)(2,1)} %bitcast.29), custom_call_target="tpu_custom_call" | custom-call | flops 60000000 | bytes 40000000 | tf_op jit(solution)/shard_map/filter_twice/pallas_call | solution.py:182
  12.4 0.9 %collective-permute-done = bf16[1,16,12,2048]{3,1,2,0:T(8,128)(2,1)S(1)} collective-permute-done((bf16[1,16,12,2048]{3,1,2,0:T(8,128)(2,1)}, bf16[1,16,12,2048]{3,1,2,0:T(8,128)(2,1)S(1)}, u32[]{:S(2)}, u32[]{:S(2)}) %collective-permute-start) | collective-permute-done | bytes 786464 | tf_op jit(solution)/shard_map/ppermute | solution.py:303
  13.2 0.0 copy-start.1
  13.2 15.7 %all-to-all-start = ((bf16[256,4,256]{2,1,0:T(4,128)(2,1)}), bf16[256,4,256]{2,1,0:T(4,128)(2,1)S(1)}, u32[]{:S(2)}, u32[]{:S(2)}) async-start(bf16[256,4,256]{2,1,0:T(4,128)(2,1)} %bitcast.27), calls=%async_computation | async-start | bytes 1048576 | tf_op jit(solution)/shard_map/all_to_all | solution.py:312
  28.9 0.0 copy-done.3
  28.9 0.1 copy.8
  29.0 0.1 eq.32
  29.1 0.1 and_convert_fusion.place_ref
  29.2 0.0 copy-done.1
  29.2 0.0 copy-done
  29.3 0.0 copy-start.2
  29.3 1.1 %copy-done.2 = bf16[1,16,12,2048]{3,1,2,0:T(8,128)(2,1)S(1)} copy-done((bf16[1,16,12,2048]{3,1,2,0:T(8,128)(2,1)S(1)}, bf16[1,16,12,2048]{3,1,2,0:T(8,128)(2,1)}, u32[]{:S(2)}) %copy-start.2) | copy-done | bytes 786456
  30.4 6.3 %spread_blocks.1.mixer_ref = bf16[1024,1024]{1,0:T(8,128)(2,1)S(1)} custom-call(s32[1]{0:T(128)} %bitcast.half_ref, bf16[256,192]{1,0:T(8,128)(2,1)S(1)} %and_convert_fusion.place_ref, bf16[192,2048]{1,0:T(8,128)(2,1)S(1)} %bitcast.25, bf16[192,2048]{1,0:T(8,128)(2,1)S(1)} %bitcast.26), custom_call_target="tpu_custom_call" | custom-call | flops 400000000 | bytes 15000000 | tf_op jit(solution)/shard_map/spread_blocks/pallas_call | solution.py:276
  36.7 12.6 %all-to-all-done = bf16[256,4,256]{2,1,0:T(4,128)(2,1)S(1)} async-done(((bf16[256,4,256]{2,1,0:T(4,128)(2,1)}), bf16[256,4,256]{2,1,0:T(4,128)(2,1)S(1)}, u32[]{:S(2)}, u32[]{:S(2)}) %all-to-all-start) | async-done | bytes 524320 | tf_op jit(solution)/shard_map/all_to_all | solution.py:312
  49.3 0.1 reshape.105.points_ref
  49.5 1.5 %mix_twice.1 = bf16[1024,256]{1,0:T(8,128)(2,1)S(1)} custom-call(bf16[1024,1024]{1,0:T(8,128)(2,1)S(1)} %spread_blocks.1.mixer_ref, bf16[1024,256]{1,0:T(8,128)(2,1)S(1)} %reshape.105.points_ref), custom_call_target="tpu_custom_call" | custom-call | flops 1100000000 | bytes 4000000 | tf_op jit(solution)/shard_map/mix_twice/pallas_call | solution.py:218
  51.0 0.1 reshape.106
  51.1 26.9 %all_to_all.10 = bf16[256,4,256]{2,1,0:T(4,128)(2,1)S(1)} all-to-all(bf16[256,4,256]{2,1,0:T(4,128)(2,1)S(1)} %reshape.106), channel_id=1, replica_groups=mesh['wide'=128,'narrow'=2] {'narrow','wide'}, dimensions={0} | all-to-all | bytes 1048576 | tf_op jit(solution)/shard_map/all_to_all | solution.py:314
  78.0 0.8 %copy.12 = bf16[4,65536]{1,0:T(4,128)(2,1)} copy(bf16[4,65536]{1,0:T(4,128)(2,1)S(1)} %bitcast.28) | data formatting | bytes 1048576
  (2 shorter events, 0.0 us)
Async XLA Ops:
  0.0 29.3 %copy-start = (bf16[1,16,12,2048]{3,1,2,0:T(8,128)(2,1)S(1)}, bf16[1,16,12,2048]{3,1,2,0:T(8,128)(2,1)}, u32[]{:S(2)}) copy-start(bf16[1,16,12,2048]{3,1,2,0:T(8,128)(2,1)} %param.9) | copy-start | bytes 2359300
  0.0 28.9 %copy-start.3 = (s32[16,12]{1,0:T(8,128)S(1)}, s32[16,12]{1,0:T(8,128)}, u32[]{:S(2)}) copy-start(s32[16,12]{1,0:T(8,128)} %param.8) | copy-start | bytes 2308
  0.0 13.2 %collective-permute-start = (bf16[1,16,12,2048]{3,1,2,0:T(8,128)(2,1)}, bf16[1,16,12,2048]{3,1,2,0:T(8,128)(2,1)S(1)}, u32[]{:S(2)}, u32[]{:S(2)}) collective-permute-start(bf16[1,16,12,2048]{3,1,2,0:T(8,128)(2,1)} %param.9), channel_id=1, source_target_pairs={{1,0},{32,1},{35,2},{2,3},{5,4},{36,5},{39,6},{6,7},{9,8},{40,9},{... | collective-permute-start | bytes 2359304 | tf_op jit(solution)/shard_map/ppermute | solution.py:303
  13.2 16.0 %copy-start.1 = (bf16[1,16,12,2048]{3,1,2,0:T(8,128)(2,1)}, bf16[1,16,12,2048]{3,1,2,0:T(8,128)(2,1)S(1)}, u32[]{:S(2)}) copy-start(bf16[1,16,12,2048]{3,1,2,0:T(8,128)(2,1)S(1)} %collective-permute-done) | copy-start | bytes 2359300
  13.2 36.1 %all-to-all-start = ((bf16[256,4,256]{2,1,0:T(4,128)(2,1)}), bf16[256,4,256]{2,1,0:T(4,128)(2,1)S(1)}, u32[]{:S(2)}, u32[]{:S(2)}) async-start(bf16[256,4,256]{2,1,0:T(4,128)(2,1)} %bitcast.27), calls=%async_computation | async-start | bytes 1048576 | tf_op jit(solution)/shard_map/all_to_all | solution.py:312
  29.3 1.1 %copy-start.2 = (bf16[1,16,12,2048]{3,1,2,0:T(8,128)(2,1)S(1)}, bf16[1,16,12,2048]{3,1,2,0:T(8,128)(2,1)}, u32[]{:S(2)}) copy-start(bf16[1,16,12,2048]{3,1,2,0:T(8,128)(2,1)} %copy-done.1) | copy-start | bytes 2359300

commit v5 on v4

--- a/solution.py
+++ b/solution.py
@@ -202,43 +202,45 @@
     )(coefficient, potential, rows)
 
 
-def mix_kernel(mixer_ref, points_ref, out_ref, middle_ref):
+def mix_kernel(half_ref, own_ref, other_ref, points_ref, out_ref, first_ref, middle_ref):
     size = points_ref.shape[1]
-    points = jnp.dot(points_ref[...], point_order(size), preferred_element_type=jnp.float32).astype(jnp.bfloat16)
-    for start in range(0, FUNCS, size):
-        part = jnp.dot(mixer_ref[start:start + size, :], points, preferred_element_type=jnp.float32)
-        middle_ref[start:start + size, :] = part.astype(jnp.bfloat16)
-    points = middle_ref[...]
-    for start in range(0, FUNCS, size):
-        part = jnp.dot(mixer_ref[start:start + size, :], points, preferred_element_type=jnp.float32)
-        out_ref[start:start + size, :] = part.astype(jnp.bfloat16)
-
-
-def mix_twice(mixer, points):
+    points = jnp.dot(points_ref[...], point_order(size), preferred_element_type=jnp.float32)
+    first_ref[...] = points.astype(jnp.bfloat16)
+    count = FUNCS // 2
+    for source_ref, target_ref in ((first_ref, middle_ref), (middle_ref, out_ref)):
+        own = source_ref[pl.ds(pl.multiple_of(half_ref[0] * count, count), count), :]
+        other = source_ref[pl.ds(pl.multiple_of((1 - half_ref[0]) * count, count), count), :]
+        for start in range(0, FUNCS, size):
+            rows = slice(start, start + size)
+            part = jnp.dot(own_ref[rows, :], own, preferred_element_type=jnp.float32)
+            part = part + jnp.dot(other_ref[rows, :], other, preferred_element_type=jnp.float32)
+            target_ref[rows, :] = part.astype(jnp.bfloat16)
+
+
+def mix_twice(half, own, other, points):
     return pl.pallas_call(
         mix_kernel,
         name="mix_twice",
         out_shape=jax.ShapeDtypeStruct(points.shape, jnp.bfloat16),
-        in_specs=[pl.BlockSpec(memory_space=pltpu.VMEM)] * 2,
+        in_specs=[pl.BlockSpec(memory_space=pltpu.SMEM)] + [pl.BlockSpec(memory_space=pltpu.VMEM)] * 3,
         out_specs=pl.BlockSpec(memory_space=pltpu.VMEM),
-        scratch_shapes=[pltpu.VMEM(points.shape, jnp.bfloat16)],
+        scratch_shapes=[pltpu.VMEM(points.shape, jnp.bfloat16)] * 2,
         compiler_params=pltpu.CompilerParams(vmem_limit_bytes=24 * 2**20),
         cost_estimate=pl.CostEstimate(flops=1_100_000_000, bytes_accessed=4_000_000, transcendentals=0),
-    )(mixer, points)
-
-
-def spread_kernel(half_ref, place_ref, own_ref, other_ref, out_ref, wide_ref):
+    )(half, own, other, points)
+
+
+def spread_kernel(place_ref, *refs):
+    *source_refs, out_ref, wide_ref = refs
     lane = lax.broadcasted_iota(jnp.int32, (SUBLANES, LANES), 1)
     row_blocks = FUNCS // BLOCK
     column_tiles = FUNCS // 2 // LANES
-    sides = ((own_ref, half_ref[0]), (other_ref, 1 - half_ref[0]))
-
-    def one_pair(pair, carry):
-        columns = pl.ds(pl.multiple_of(pair * 2 * LANES, 2 * LANES), 2 * LANES)
-        spreads = []
-        for source_ref, _ in sides:
-            spreads.append(jnp.dot(place_ref[...], source_ref[:, columns], preferred_element_type=jnp.float32))
-        for spread, (_, half) in zip(spreads, sides):
+
+    def one_pair(index, carry):
+        for pair in (2 * index, 2 * index + 1):
+            columns = pl.ds(pl.multiple_of(pair * 2 * LANES, 2 * LANES), 2 * LANES)
+            entries = jnp.concatenate([source_ref[:, columns] for source_ref in source_refs], 0)
+            spread = jnp.dot(place_ref[...], entries, preferred_element_type=jnp.float32)
             for side in range(2):
                 for tile in range(column_tiles):
                     for rows in range(row_blocks // SUBLANES):
@@ -251,38 +253,47 @@
                             for step in range(4)
                         ]
                         for fun, value in enumerate(swap_chunks(group, lane)):
-                            start = (half * column_tiles + tile) * FUNCS
-                            start = start + side * (FUNCS // 2) + rows * SUBLANES * (BLOCK // 2) + pair * FUN_DEV + fun
+                            start = tile * FUNCS + side * (FUNCS // 2)
+                            start = start + rows * SUBLANES * (BLOCK // 2) + pair * FUN_DEV + fun
                             wide_ref[pl.ds(start, SUBLANES, stride=BLOCK // 2), :] = value
         return carry
 
-    lax.fori_loop(0, BLOCK * BLOCK // 2 // (2 * LANES), one_pair, 0)
-    for tile in range(FUNCS // LANES):
+    lax.fori_loop(0, BLOCK * BLOCK // 2 // (4 * LANES), one_pair, 0)
+    for tile in range(column_tiles):
         out_ref[:, tile * LANES:(tile + 1) * LANES] = wide_ref[tile * FUNCS:(tile + 1) * FUNCS, :].astype(jnp.bfloat16)
 
 
-def dense_mixer(half, own, other, block_cols):
+def spread_blocks(place, *sources):
+    return pl.pallas_call(
+        spread_kernel,
+        name="spread_blocks",
+        out_shape=jax.ShapeDtypeStruct((FUNCS, FUNCS // 2), jnp.bfloat16),
+        in_specs=[pl.BlockSpec(memory_space=pltpu.VMEM)] * (1 + len(sources)),
+        out_specs=pl.BlockSpec(memory_space=pltpu.VMEM),
+        scratch_shapes=[pltpu.VMEM((FUNCS * FUNCS // 2 // LANES, LANES), jnp.float32)],
+        compiler_params=pltpu.CompilerParams(vmem_limit_bytes=60 * 2**20),
+        cost_estimate=pl.CostEstimate(flops=200_000_000, bytes_accessed=8_000_000, transcendentals=0),
+    )(place, *sources)
+
+
+def dense_halves(core, own, near, far, block_cols):
     row_blocks, slots = block_cols.shape
     entry = jnp.arange(slots * row_blocks)
     place = jnp.arange(row_blocks * row_blocks)
     column = block_cols.T.reshape(-1)
-    chosen = (column[None, :] == place[:, None] // row_blocks) & (
-        entry[None, :] % row_blocks == place[:, None] % row_blocks
-    )
+    cut = column.shape[0] // 2
+    swapped = jnp.where(core == 0, column, jnp.concatenate([column[cut:], column[:cut]]))
+
+    def chosen(column):
+        return (
+            (column[None, :] == place[:, None] // row_blocks)
+            & (entry[None, :] % row_blocks == place[:, None] % row_blocks)
+        ).astype(jnp.bfloat16)
 
     def flat(blocks):
-        return blocks[0].transpose(1, 0, 2).reshape(slots * row_blocks, BLOCK * BLOCK // 2)
-
-    return pl.pallas_call(
-        spread_kernel,
-        name="spread_blocks",
-        out_shape=jax.ShapeDtypeStruct((FUNCS, FUNCS), jnp.bfloat16),
-        in_specs=[pl.BlockSpec(memory_space=pltpu.SMEM)] + [pl.BlockSpec(memory_space=pltpu.VMEM)] * 3,
-        out_specs=pl.BlockSpec(memory_space=pltpu.VMEM),
-        scratch_shapes=[pltpu.VMEM((FUNCS * FUNCS // LANES, LANES), jnp.float32)],
-        compiler_params=pltpu.CompilerParams(vmem_limit_bytes=16 * 2**20),
-        cost_estimate=pl.CostEstimate(flops=400_000_000, bytes_accessed=15_000_000, transcendentals=0),
-    )(half.reshape(1), chosen.astype(jnp.bfloat16), flat(own), flat(other))
+        return blocks[0].transpose(1, 0, 2).reshape(-1, BLOCK * BLOCK // 2)
+
+    return spread_blocks(chosen(column), flat(own)), spread_blocks(chosen(swapped), flat(near), flat(far))
 
 
 def other_half_pairs(wide, narrow):
@@ -300,17 +311,21 @@
 def local(functions, potential, cheb_coef, block_cols, kernel_halves):
     devices = lax.axis_size("wide") * lax.axis_size("narrow")
     own = GRID // devices
-    other = lax.ppermute(
-        kernel_halves, ("wide", "narrow"), other_half_pairs(lax.axis_size("wide"), lax.axis_size("narrow"))
-    )
+    wide, narrow = lax.axis_size("wide"), lax.axis_size("narrow")
+    core = lax.axis_index("wide") % 2
+    slots = kernel_halves.shape[2] // 2
+    part = lax.dynamic_slice_in_dim(kernel_halves, core * slots, slots, 2)
+    near = lax.ppermute(part, ("wide", "narrow"), other_half_pairs(wide, narrow))
     rows = functions.reshape(FUN_DEV, TILES, LANES).transpose(1, 0, 2).reshape(TILES * FUN_DEV, LANES)
     filtered = filter_twice(rows, potential, cheb_coef)
-    filtered, other = lax.optimization_barrier((filtered, other))
-    mixer = dense_mixer(lax.axis_index("narrow"), kernel_halves, other, block_cols)
+    filtered, near = lax.optimization_barrier((filtered, near))
+    far = lax.ppermute(near, "wide", [(index, index ^ 1) for index in range(wide)])
+    mixers = dense_halves(core, kernel_halves, near, far, block_cols)
     outgoing = filtered.reshape(devices, own // LANES, FUN_DEV, LANES).transpose(0, 2, 1, 3)
     outgoing = outgoing.reshape(devices, FUN_DEV, own)
     points = lax.all_to_all(outgoing, ("narrow", "wide"), split_axis=0, concat_axis=0, tiled=True)
-    mixed = mix_twice(mixer, points.reshape(FUNCS, own))
+    half = lax.axis_index("narrow").reshape(1)
+    mixed = mix_twice(half, *mixers, points.reshape(FUNCS, own))
     result = lax.all_to_all(
         mixed.reshape(devices, FUN_DEV, own), ("narrow", "wide"), split_axis=0, concat_axis=0, tiled=True
     )

time: 79 us -> 78.8 us (level)
  waiting for transfers between devices: 13.5 us -> 5.5 us
  Pallas kernels: 18 us -> 22.4 us
  local copies, waits for them, and re-layouts: 2.34 us -> 3.4 us
  other arithmetic: 0.15 us -> 0.97 us
    all_to_all x1, waiting for transfers between devices: 12.6 us -> 5.49 us  [local(): lax.all_to_all(outgoing, ('narrow', 'wide'), split_axis=0, concat_axis=0,...]
    pallas_call x1 -> x2, Pallas kernels: 6.34 us -> 10.5 us  [spread_blocks(): pl.pallas_call(spread_kernel, name='spread_blocks', out_shape=jax.ShapeDt...]
    ppermute x1 -> x2, starting transfers between devices: 2.13 us -> 4.38 us  [the longest x1 2.2 us: local(): lax.ppermute(part, ('wide', 'narrow'), other_half_pairs(wide, narrow))]
    all_to_all x1, starting transfers between devices: 15.7 us -> 14.1 us  [local(): lax.all_to_all(outgoing, ('narrow', 'wide'), split_axis=0, concat_axis=0,...]
    dynamic_slice x0 -> x1, local copies, waits for them, and re-layouts: none -> 1.02 us  [local(): part = lax.dynamic_slice_in_dim(kernel_halves, core * slots, slots, 2)]
    ppermute x1 -> x2, waiting for transfers between devices: 0.85 us -> 0.01 us  [the longest x1 0.01 us: local(): lax.ppermute(part, ('wide', 'narrow'), other_half_pairs(wide, narrow))]
    unnamed x9 -> x11, local copies, waits for them, and re-layouts: 1.93 us -> 1.57 us
  transfers between devices with their start and end apart: 2 -> 3, of which waited for: 2 -> 1; matrix products, arithmetic and copies ran while one was open for 0% -> 2% of each run, Pallas kernels for 21% -> 26%
where the time goes in v5:
time: 78.8 us; the launch traced here: 78.4 us
  blocking collectives  27.5 us (35%)
  Pallas kernels  22.4 us (28%)
  starting transfers between devices  18.5 us (23%)
  waiting for transfers between devices  5.5 us (7%)
  local copies, waits for them, and re-layouts  3.4 us (4%)
  other arithmetic  0.97 us (1%)
    all_to_all x1, blocking collectives, local(): lax.all_to_all(mixed.reshape(devices, FUN_DEV, own), ('narrow', 'wide'),...  27.5 us
    all_to_all x1, starting transfers between devices, local(): lax.all_to_all(outgoing, ('narrow', 'wide'), split_axis=0, concat_axis=0,...  14.1 us
    pallas_call x2, Pallas kernels, spread_blocks(): pl.pallas_call(spread_kernel, name='spread_blocks', out_shape=jax.ShapeDt...  10.5 us
    pallas_call x1, Pallas kernels, filter_twice(): pl.pallas_call(filter_kernel, name='filter_twice', out_shape=jax.ShapeDty...  10.2 us
    all_to_all x1, waiting for transfers between devices, local(): lax.all_to_all(outgoing, ('narrow', 'wide'), split_axis=0, concat_axis=0,...  5.49 us
    ppermute x1, starting transfers between devices, local(): lax.ppermute(part, ('wide', 'narrow'), other_half_pairs(wide, narrow))  2.2 us
    ppermute x1, starting transfers between devices, local(): lax.ppermute(near, 'wide', [(index, index ^ 1) for index in range(wide)])  2.18 us
    pallas_call x1, Pallas kernels, mix_twice(): pl.pallas_call(mix_kernel, name='mix_twice', out_shape=jax.ShapeDtypeStru...  1.74 us
  transfers between devices with their start and end apart: 3, of which 1 were waited for; matrix products, arithmetic and copies ran while one was open for 2% of the time, Pallas kernels for 26%

profile of v5, /device:TPU:1, one launch (start us, length us, event | category | flops | bytes accessed | tf_op | source)
XLA Modules:
  0.0 78.4 jit_solution(5845148724739083896)
XLA Ops:
  0.0 1.0 %constant_dynamic-slice_fusion = bf16[1,16,6,2048]{3,1,2,0:T(8,128)(2,1)S(1)} fusion(bf16[1,16,12,2048]{3,1,2,0:T(8,128)(2,1)} %param.9, s32[]{:T(128)S(6)} %select_n.71), kind=kLoop, calls=%fused_computation.13 | loop fusion | bytes 786436 | tf_op jit(solution)/shard_map/dynamic_slice | solution.py:317
  1.0 2.2 %collective-permute-start = (bf16[1,16,6,2048]{3,1,2,0:T(8,128)(2,1)S(1)}, bf16[1,16,6,2048]{3,1,2,0:T(8,128)(2,1)S(1)}, u32[]{:S(2)}, u32[]{:S(2)}) collective-permute-start(bf16[1,16,6,2048]{3,1,2,0:T(8,128)(2,1)S(1)} %constant_dynamic-slice_fusion), channel_id=1, source_target_pairs={{1,0},{32,1},{35,2},{2,3},{5,4},{36,5},{39,6},{6,7},{9,8},{40,9},{... | collective-permute-start | bytes 1179656 | tf_op jit(solution)/shard_map/ppermute | solution.py:318
  3.2 10.2 %filter_twice.1 = bf16[2048,128]{1,0:T(8,128)(2,1)} custom-call(f32[9]{0:T(128)} %coef_hbm.1, f32[64,1024]{1,0:T(8,128)} %potential_hbm.1, bf16[2048,128]{1,0:T(8,128)(2,1)} %bitcast.33), custom_call_target="tpu_custom_call" | custom-call | flops 60000000 | bytes 40000000 | tf_op jit(solution)/shard_map/filter_twice/pallas_call | solution.py:182
  13.5 0.0 collective-permute-done
  13.5 0.0 copy-start.2
  13.5 0.0 copy-start.4
  13.5 14.1 %all-to-all-start = ((bf16[256,4,256]{2,1,0:T(4,128)(2,1)}), bf16[256,4,256]{2,1,0:T(4,128)(2,1)S(1)}, u32[]{:S(2)}, u32[]{:S(2)}) async-start(bf16[256,4,256]{2,1,0:T(4,128)(2,1)} %bitcast.30), calls=%async_computation | async-start | bytes 1048576 | tf_op jit(solution)/shard_map/all_to_all | solution.py:326
  27.6 0.0 copy-done.4
  27.6 0.1 copy.10
  27.7 0.1 eq.65
  27.8 0.1 fusion.4
  27.9 0.1 copy.11
  27.9 0.1 concatenate.11
  28.0 0.1 copy.12
  28.1 0.1 concatenate.12
  28.2 0.1 add_select_fusion
  28.3 0.0 copy-done.2
  28.3 2.2 %collective-permute-start.1 = (bf16[1,16,6,2048]{3,1,2,0:T(8,128)(2,1)S(1)}, bf16[1,16,6,2048]{3,1,2,0:T(8,128)(2,1)S(1)}, u32[]{:S(2)}, u32[]{:S(2)}) collective-permute-start(bf16[1,16,6,2048]{3,1,2,0:T(8,128)(2,1)S(1)} %collective-permute-done), channel_id=1, source_target_pairs={{0,2},{2,0},{4,6},{6,4},{8,10},{10,8},{12,14},{14,12},{16,18},{18,... | collective-permute-start | bytes 1179656 | tf_op jit(solution)/shard_map/ppermute | solution.py:322
  30.5 0.9 %fusion.1 = (bf16[256,192]{1,0:T(8,128)(2,1)}, bf16[256,192]{1,0:T(8,128)(2,1)}) fusion(s32[192]{0:T(256)S(1)} %add_select_fusion, s32[192]{0:T(256)S(1)} %and_select_fusion.1, s32[256]{0:T(256)S(1)} %get-tuple-element.13, s32[256]{0:T(256)S(1)} %get-tuple-element.14, s32[192]{0:T(256)S(1)} %eq.65), kind=kLoop, calls=%fused_computation.3 | loop fusion | flops 344064 | bytes 200960 | tf_op jit(solution)/shard_map/convert_element_type | solution.py:291
  31.3 5.2 %spread_blocks.2.own_ref = bf16[1024,512]{1,0:T(8,128)(2,1)} custom-call(bf16[256,192]{1,0:T(8,128)(2,1)} %get-tuple-element.12.place_ref, bf16[192,2048]{1,0:T(8,128)(2,1)} %bitcast.32), custom_call_target="tpu_custom_call" | custom-call | flops 200000000 | bytes 8000000 | tf_op jit(solution)/shard_map/spread_blocks/pallas_call | solution.py:267
  36.5 0.0 collective-permute-done.1
  36.5 0.0 copy-start.3
  36.5 0.8 copy-done.3
  37.3 0.0 copy-start
  37.3 5.3 %spread_blocks.3.other_ref = bf16[1024,512]{1,0:T(8,128)(2,1)} custom-call(bf16[256,192]{1,0:T(8,128)(2,1)} %get-tuple-element.11.place_ref, bf16[96,2048]{1,0:T(8,128)(2,1)} %bitcast.34, bf16[96,2048]{1,0:T(8,128)(2,1)} %bitcast.35), custom_call_target="tpu_custom_call" | custom-call | flops 200000000 | bytes 8000000 | tf_op jit(solution)/shard_map/spread_blocks/pallas_call | solution.py:267
  42.6 0.0 copy-start.1
  42.6 5.5 %all-to-all-done = bf16[256,4,256]{2,1,0:T(4,128)(2,1)S(1)} async-done(((bf16[256,4,256]{2,1,0:T(4,128)(2,1)}), bf16[256,4,256]{2,1,0:T(4,128)(2,1)S(1)}, u32[]{:S(2)}, u32[]{:S(2)}) %all-to-all-start) | async-done | bytes 524320 | tf_op jit(solution)/shard_map/all_to_all | solution.py:326
  48.1 0.1 reshape.133.points_ref
  48.2 0.0 copy-done
  48.2 0.0 copy-done.1
  48.2 1.7 %mix_twice.1 = bf16[1024,256]{1,0:T(8,128)(2,1)S(1)} custom-call(s32[1]{0:T(128)} %bitcast.half_ref, bf16[1024,512]{1,0:T(8,128)(2,1)S(1)} %copy-done, bf16[1024,512]{1,0:T(8,128)(2,1)S(1)} %copy-done.1, bf16[1024,256]{1,0:T(8,128)(2,1)S(1)} %reshape.133.points_ref), custom_call_target="tpu_custom_call" | custom-call | flops 1100000000 | bytes 4000000 | tf_op jit(solution)/shard_map/mix_twice/pallas_call | solution.py:221
  49.9 0.1 reshape.134
  50.1 27.5 %all_to_all.10 = bf16[256,4,256]{2,1,0:T(4,128)(2,1)S(1)} all-to-all(bf16[256,4,256]{2,1,0:T(4,128)(2,1)S(1)} %reshape.134), channel_id=1, replica_groups=mesh['wide'=128,'narrow'=2] {'narrow','wide'}, dimensions={0} | all-to-all | bytes 1048576 | tf_op jit(solution)/shard_map/all_to_all | solution.py:329
  77.6 0.8 %copy.16 = bf16[4,65536]{1,0:T(4,128)(2,1)} copy(bf16[4,65536]{1,0:T(4,128)(2,1)S(1)} %bitcast.31) | data formatting | bytes 1048576
  (2 shorter events, 0.0 us)
Async XLA Ops:
  1.0 12.4 %collective-permute-start = (bf16[1,16,6,2048]{3,1,2,0:T(8,128)(2,1)S(1)}, bf16[1,16,6,2048]{3,1,2,0:T(8,128)(2,1)S(1)}, u32[]{:S(2)}, u32[]{:S(2)}) collective-permute-start(bf16[1,16,6,2048]{3,1,2,0:T(8,128)(2,1)S(1)} %constant_dynamic-slice_fusion), channel_id=1, source_target_pairs={{1,0},{32,1},{35,2},{2,3},{5,4},{36,5},{39,6},{6,7},{9,8},{40,9},{... | collective-permute-start | bytes 1179656 | tf_op jit(solution)/shard_map/ppermute | solution.py:318
  13.5 14.8 %copy-start.2 = (bf16[1,16,6,2048]{3,1,2,0:T(8,128)(2,1)}, bf16[1,16,6,2048]{3,1,2,0:T(8,128)(2,1)S(1)}, u32[]{:S(2)}) copy-start(bf16[1,16,6,2048]{3,1,2,0:T(8,128)(2,1)S(1)} %collective-permute-done) | copy-start | bytes 1179652
  13.5 14.1 %copy-start.4 = (s32[16,12]{1,0:T(8,128)S(1)}, s32[16,12]{1,0:T(8,128)}, u32[]{:S(2)}) copy-start(s32[16,12]{1,0:T(8,128)} %param.8) | copy-start | bytes 2308
  13.5 34.6 %all-to-all-start = ((bf16[256,4,256]{2,1,0:T(4,128)(2,1)}), bf16[256,4,256]{2,1,0:T(4,128)(2,1)S(1)}, u32[]{:S(2)}, u32[]{:S(2)}) async-start(bf16[256,4,256]{2,1,0:T(4,128)(2,1)} %bitcast.30), calls=%async_computation | async-start | bytes 1048576 | tf_op jit(solution)/shard_map/all_to_all | solution.py:326
  28.3 8.2 %collective-permute-start.1 = (bf16[1,16,6,2048]{3,1,2,0:T(8,128)(2,1)S(1)}, bf16[1,16,6,2048]{3,1,2,0:T(8,128)(2,1)S(1)}, u32[]{:S(2)}, u32[]{:S(2)}) collective-permute-start(bf16[1,16,6,2048]{3,1,2,0:T(8,128)(2,1)S(1)} %collective-permute-done), channel_id=1, source_target_pairs={{0,2},{2,0},{4,6},{6,4},{8,10},{10,8},{12,14},{14,12},{16,18},{18,... | collective-permute-start | bytes 1179656 | tf_op jit(solution)/shard_map/ppermute | solution.py:322
  36.5 0.8 copy-start.3
  37.3 10.9 %copy-start = (bf16[1024,512]{1,0:T(8,128)(2,1)S(1)}, bf16[1024,512]{1,0:T(8,128)(2,1)}, u32[]{:S(2)}) copy-start(bf16[1024,512]{1,0:T(8,128)(2,1)} %spread_blocks.2.own_ref) | copy-start | bytes 3145732
  42.6 5.6 %copy-start.1 = (bf16[1024,512]{1,0:T(8,128)(2,1)S(1)}, bf16[1024,512]{1,0:T(8,128)(2,1)}, u32[]{:S(2)}) copy-start(bf16[1024,512]{1,0:T(8,128)(2,1)} %spread_blocks.3.other_ref) | copy-start | bytes 3145732

commit v6 on v5

--- a/solution.py
+++ b/solution.py
@@ -230,7 +230,7 @@
     )(half, own, other, points)
 
 
-def spread_kernel(place_ref, *refs):
+def spread_kernel(core_ref, place_ref, *refs):
     *source_refs, out_ref, wide_ref = refs
     lane = lax.broadcasted_iota(jnp.int32, (SUBLANES, LANES), 1)
     row_blocks = FUNCS // BLOCK
@@ -239,7 +239,10 @@
     def one_pair(index, carry):
         for pair in (2 * index, 2 * index + 1):
             columns = pl.ds(pl.multiple_of(pair * 2 * LANES, 2 * LANES), 2 * LANES)
-            entries = jnp.concatenate([source_ref[:, columns] for source_ref in source_refs], 0)
+            parts = [source_ref[:, columns] for source_ref in source_refs]
+            entries = jnp.concatenate(parts, 0)
+            if len(parts) > 1:
+                entries = jnp.where(core_ref[0] == 0, entries, jnp.concatenate(parts[::-1], 0))
             spread = jnp.dot(place_ref[...], entries, preferred_element_type=jnp.float32)
             for side in range(2):
                 for tile in range(column_tiles):
@@ -263,17 +266,17 @@
         out_ref[:, tile * LANES:(tile + 1) * LANES] = wide_ref[tile * FUNCS:(tile + 1) * FUNCS, :].astype(jnp.bfloat16)
 
 
-def spread_blocks(place, *sources):
+def spread_blocks(vmem, core, place, *sources):
     return pl.pallas_call(
         spread_kernel,
         name="spread_blocks",
         out_shape=jax.ShapeDtypeStruct((FUNCS, FUNCS // 2), jnp.bfloat16),
-        in_specs=[pl.BlockSpec(memory_space=pltpu.VMEM)] * (1 + len(sources)),
+        in_specs=[pl.BlockSpec(memory_space=pltpu.SMEM)] + [pl.BlockSpec(memory_space=pltpu.VMEM)] * (1 + len(sources)),
         out_specs=pl.BlockSpec(memory_space=pltpu.VMEM),
         scratch_shapes=[pltpu.VMEM((FUNCS * FUNCS // 2 // LANES, LANES), jnp.float32)],
-        compiler_params=pltpu.CompilerParams(vmem_limit_bytes=60 * 2**20),
+        compiler_params=pltpu.CompilerParams(vmem_limit_bytes=vmem * 2**20),
         cost_estimate=pl.CostEstimate(flops=200_000_000, bytes_accessed=8_000_000, transcendentals=0),
-    )(place, *sources)
+    )(core, place, *sources)
 
 
 def dense_halves(core, own, near, far, block_cols):
@@ -281,19 +284,16 @@
     entry = jnp.arange(slots * row_blocks)
     place = jnp.arange(row_blocks * row_blocks)
     column = block_cols.T.reshape(-1)
-    cut = column.shape[0] // 2
-    swapped = jnp.where(core == 0, column, jnp.concatenate([column[cut:], column[:cut]]))
-
-    def chosen(column):
-        return (
-            (column[None, :] == place[:, None] // row_blocks)
-            & (entry[None, :] % row_blocks == place[:, None] % row_blocks)
-        ).astype(jnp.bfloat16)
+    chosen = (
+        (column[None, :] == place[:, None] // row_blocks)
+        & (entry[None, :] % row_blocks == place[:, None] % row_blocks)
+    ).astype(jnp.bfloat16)
 
     def flat(blocks):
         return blocks[0].transpose(1, 0, 2).reshape(-1, BLOCK * BLOCK // 2)
 
-    return spread_blocks(chosen(column), flat(own)), spread_blocks(chosen(swapped), flat(near), flat(far))
+    core = core.reshape(1)
+    return spread_blocks(60, core, chosen, flat(own)), spread_blocks(16, core, chosen, flat(near), flat(far))
 
 
 def other_half_pairs(wide, narrow):

time: 78.8 us -> 78 us (0.990)
  waiting for transfers between devices: 5.5 us -> 9.09 us
  Pallas kernels: 22.4 us -> 20.1 us
  local copies, waits for them, and re-layouts: 3.4 us -> 2.24 us
    all_to_all x1, waiting for transfers between devices: 5.49 us -> 9.08 us  [local(): lax.all_to_all(outgoing, ('narrow', 'wide'), split_axis=0, concat_axis=0,...]
    pallas_call x2, Pallas kernels: 10.5 us -> 8.13 us  [spread_blocks(): pl.pallas_call(spread_kernel, name='spread_blocks', out_shape=jax.ShapeDt...]
  transfers between devices with their start and end apart: 3 -> 3, of which waited for: 1 -> 1; matrix products, arithmetic and copies ran while one was open for 2% -> 1% of each run, Pallas kernels for 26% -> 24%
where the time goes in v6:
time: 78 us; the launch traced here: 77.7 us
  blocking collectives  26.9 us (34%)
  Pallas kernels  20.1 us (26%)
  starting transfers between devices  18.5 us (24%)
  waiting for transfers between devices  9.09 us (12%)
  local copies, waits for them, and re-layouts  2.24 us (3%)
  other arithmetic  0.8 us (1%)
    all_to_all x1, blocking collectives, local(): lax.all_to_all(mixed.reshape(devices, FUN_DEV, own), ('narrow', 'wide'),...  26.9 us
    all_to_all x1, starting transfers between devices, local(): lax.all_to_all(outgoing, ('narrow', 'wide'), split_axis=0, concat_axis=0,...  14.1 us
    pallas_call x1, Pallas kernels, filter_twice(): pl.pallas_call(filter_kernel, name='filter_twice', out_shape=jax.ShapeDty...  10.2 us
    all_to_all x1, waiting for transfers between devices, local(): lax.all_to_all(outgoing, ('narrow', 'wide'), split_axis=0, concat_axis=0,...  9.08 us
    pallas_call x2, Pallas kernels, spread_blocks(): pl.pallas_call(spread_kernel, name='spread_blocks', out_shape=jax.ShapeDt...  8.13 us
    ppermute x1, starting transfers between devices, local(): lax.ppermute(near, 'wide', [(index, index ^ 1) for index in range(wide)])  2.23 us
    ppermute x1, starting transfers between devices, local(): lax.ppermute(part, ('wide', 'narrow'), other_half_pairs(wide, narrow))  2.2 us
    pallas_call x1, Pallas kernels, mix_twice(): pl.pallas_call(mix_kernel, name='mix_twice', out_shape=jax.ShapeDtypeStru...  1.73 us
  transfers between devices with their start and end apart: 3, of which 1 were waited for; matrix products, arithmetic and copies ran while one was open for 1% of the time, Pallas kernels for 24%

profile of v6, /device:TPU:1, one launch (start us, length us, event | category | flops | bytes accessed | tf_op | source)
XLA Modules:
  0.0 77.7 jit_solution(10779559787429887078)
XLA Ops:
  0.0 1.0 %constant_dynamic-slice_fusion = bf16[1,16,6,2048]{3,1,2,0:T(8,128)(2,1)S(1)} fusion(bf16[1,16,12,2048]{3,1,2,0:T(8,128)(2,1)} %param.9, s32[]{:T(128)S(6)} %select_n.46), kind=kLoop, calls=%fused_computation.9 | loop fusion | bytes 786436 | tf_op jit(solution)/shard_map/dynamic_slice | solution.py:317
  1.0 2.2 %collective-permute-start = (bf16[1,16,6,2048]{3,1,2,0:T(8,128)(2,1)S(1)}, bf16[1,16,6,2048]{3,1,2,0:T(8,128)(2,1)S(1)}, u32[]{:S(2)}, u32[]{:S(2)}) collective-permute-start(bf16[1,16,6,2048]{3,1,2,0:T(8,128)(2,1)S(1)} %constant_dynamic-slice_fusion), channel_id=1, source_target_pairs={{1,0},{32,1},{35,2},{2,3},{5,4},{36,5},{39,6},{6,7},{9,8},{40,9},{... | collective-permute-start | bytes 1179656 | tf_op jit(solution)/shard_map/ppermute | solution.py:318
  3.2 10.2 %filter_twice.1 = bf16[2048,128]{1,0:T(8,128)(2,1)} custom-call(f32[9]{0:T(128)} %coef_hbm.1, f32[64,1024]{1,0:T(8,128)} %potential_hbm.1, bf16[2048,128]{1,0:T(8,128)(2,1)} %bitcast.36), custom_call_target="tpu_custom_call" | custom-call | flops 60000000 | bytes 40000000 | tf_op jit(solution)/shard_map/filter_twice/pallas_call | solution.py:182
  13.5 0.0 collective-permute-done
  13.5 0.0 copy-start.2
  13.5 14.1 %all-to-all-start = ((bf16[256,4,256]{2,1,0:T(4,128)(2,1)}), bf16[256,4,256]{2,1,0:T(4,128)(2,1)S(1)}, u32[]{:S(2)}, u32[]{:S(2)}) async-start(bf16[256,4,256]{2,1,0:T(4,128)(2,1)} %bitcast.33), calls=%async_computation | async-start | bytes 1048576 | tf_op jit(solution)/shard_map/all_to_all | solution.py:326
  27.6 2.2 %collective-permute-start.1 = (bf16[1,16,6,2048]{3,1,2,0:T(8,128)(2,1)S(1)}, bf16[1,16,6,2048]{3,1,2,0:T(8,128)(2,1)S(1)}, u32[]{:S(2)}, u32[]{:S(2)}) collective-permute-start(bf16[1,16,6,2048]{3,1,2,0:T(8,128)(2,1)S(1)} %collective-permute-done), channel_id=1, source_target_pairs={{0,2},{2,0},{4,6},{6,4},{8,10},{10,8},{12,14},{14,12},{16,18},{18,... | collective-permute-start | bytes 1179656 | tf_op jit(solution)/shard_map/ppermute | solution.py:322
  29.8 0.0 copy-done.2
  29.8 0.1 copy.8
  29.9 0.1 eq.34
  30.0 0.8 %and_convert_fusion.place_ref = bf16[256,192]{1,0:T(8,128)(2,1)} fusion(s32[192]{0:T(256)S(1)} %and_select_fusion.1, s32[192]{0:T(256)S(1)} %eq.34, s32[256]{0:T(256)S(1)} %get-tuple-element.9, s32[256]{0:T(256)S(1)} %get-tuple-element.10), kind=kLoop, calls=%fused_computation | loop fusion | flops 196608 | bytes 101888 | tf_op jit(solution)/shard_map/convert_element_type | solution.py:290
  30.8 0.0 copy-start
  30.8 5.2 %spread_blocks.2.own_ref = bf16[1024,512]{1,0:T(8,128)(2,1)} custom-call(s32[1]{0:T(128)} %bitcast.1.core_ref, bf16[256,192]{1,0:T(8,128)(2,1)} %and_convert_fusion.place_ref, bf16[192,2048]{1,0:T(8,128)(2,1)} %bitcast.35), custom_call_target="tpu_custom_call" | custom-call | flops 200000000 | bytes 8000000 | tf_op jit(solution)/shard_map/spread_blocks/pallas_call | solution.py:270
  36.0 0.0 collective-permute-done.1
  36.0 0.0 copy-done
  36.0 0.0 copy-start.1
  36.0 2.9 %spread_blocks.3.other_ref = bf16[1024,512]{1,0:T(8,128)(2,1)S(1)} custom-call(s32[1]{0:T(128)} %bitcast.1.core_ref, bf16[256,192]{1,0:T(8,128)(2,1)S(1)} %copy-done, bf16[96,2048]{1,0:T(8,128)(2,1)S(1)} %bitcast.31, bf16[96,2048]{1,0:T(8,128)(2,1)S(1)} %bitcast.32), custom_call_target="tpu_custom_call" | custom-call | flops 200000000 | bytes 8000000 | tf_op jit(solution)/shard_map/spread_blocks/pallas_call | solution.py:270
  39.0 9.1 %all-to-all-done = bf16[256,4,256]{2,1,0:T(4,128)(2,1)S(1)} async-done(((bf16[256,4,256]{2,1,0:T(4,128)(2,1)}), bf16[256,4,256]{2,1,0:T(4,128)(2,1)S(1)}, u32[]{:S(2)}, u32[]{:S(2)}) %all-to-all-start) | async-done | bytes 524320 | tf_op jit(solution)/shard_map/all_to_all | solution.py:326
  48.0 0.1 reshape.113.points_ref
  48.2 0.0 copy-done.1
  48.2 1.7 %mix_twice.1 = bf16[1024,256]{1,0:T(8,128)(2,1)S(1)} custom-call(s32[1]{0:T(128)} %bitcast.half_ref, bf16[1024,512]{1,0:T(8,128)(2,1)S(1)} %copy-done.1, bf16[1024,512]{1,0:T(8,128)(2,1)S(1)} %spread_blocks.3.other_ref, bf16[1024,256]{1,0:T(8,128)(2,1)S(1)} %reshape.113.points_ref), custom_call_target="tpu_custom_call" | custom-call | flops 1100000000 | bytes 4000000 | tf_op jit(solution)/shard_map/mix_twice/pallas_call | solution.py:221
  49.9 0.1 reshape.114
  50.0 26.9 %all_to_all.10 = bf16[256,4,256]{2,1,0:T(4,128)(2,1)S(1)} all-to-all(bf16[256,4,256]{2,1,0:T(4,128)(2,1)S(1)} %reshape.114), channel_id=1, replica_groups=mesh['wide'=128,'narrow'=2] {'narrow','wide'}, dimensions={0} | all-to-all | bytes 1048576 | tf_op jit(solution)/shard_map/all_to_all | solution.py:329
  76.9 0.8 %copy.12 = bf16[4,65536]{1,0:T(4,128)(2,1)} copy(bf16[4,65536]{1,0:T(4,128)(2,1)S(1)} %bitcast.34) | data formatting | bytes 1048576
  (2 shorter events, 0.0 us)
Async XLA Ops:
  1.0 12.4 %collective-permute-start = (bf16[1,16,6,2048]{3,1,2,0:T(8,128)(2,1)S(1)}, bf16[1,16,6,2048]{3,1,2,0:T(8,128)(2,1)S(1)}, u32[]{:S(2)}, u32[]{:S(2)}) collective-permute-start(bf16[1,16,6,2048]{3,1,2,0:T(8,128)(2,1)S(1)} %constant_dynamic-slice_fusion), channel_id=1, source_target_pairs={{1,0},{32,1},{35,2},{2,3},{5,4},{36,5},{39,6},{6,7},{9,8},{40,9},{... | collective-permute-start | bytes 1179656 | tf_op jit(solution)/shard_map/ppermute | solution.py:318
  13.5 16.4 %copy-start.2 = (s32[16,12]{1,0:T(8,128)S(1)}, s32[16,12]{1,0:T(8,128)}, u32[]{:S(2)}) copy-start(s32[16,12]{1,0:T(8,128)} %param.8) | copy-start | bytes 2308
  13.5 34.6 %all-to-all-start = ((bf16[256,4,256]{2,1,0:T(4,128)(2,1)}), bf16[256,4,256]{2,1,0:T(4,128)(2,1)S(1)}, u32[]{:S(2)}, u32[]{:S(2)}) async-start(bf16[256,4,256]{2,1,0:T(4,128)(2,1)} %bitcast.33), calls=%async_computation | async-start | bytes 1048576 | tf_op jit(solution)/shard_map/all_to_all | solution.py:326
  27.6 8.4 %collective-permute-start.1 = (bf16[1,16,6,2048]{3,1,2,0:T(8,128)(2,1)S(1)}, bf16[1,16,6,2048]{3,1,2,0:T(8,128)(2,1)S(1)}, u32[]{:S(2)}, u32[]{:S(2)}) collective-permute-start(bf16[1,16,6,2048]{3,1,2,0:T(8,128)(2,1)S(1)} %collective-permute-done), channel_id=1, source_target_pairs={{0,2},{2,0},{4,6},{6,4},{8,10},{10,8},{12,14},{14,12},{16,18},{18,... | collective-permute-start | bytes 1179656 | tf_op jit(solution)/shard_map/ppermute | solution.py:322
  30.8 5.2 %copy-start = (bf16[256,192]{1,0:T(8,128)(2,1)S(1)}, bf16[256,192]{1,0:T(8,128)(2,1)}, u32[]{:S(2)}) copy-start(bf16[256,192]{1,0:T(8,128)(2,1)} %and_convert_fusion.place_ref) | copy-start | bytes 294916
  36.0 12.2 %copy-start.1 = (bf16[1024,512]{1,0:T(8,128)(2,1)S(1)}, bf16[1024,512]{1,0:T(8,128)(2,1)}, u32[]{:S(2)}) copy-start(bf16[1024,512]{1,0:T(8,128)(2,1)} %spread_blocks.2.own_ref) | copy-start | bytes 3145732

commit v7 on v6

--- a/solution.py
+++ b/solution.py
@@ -279,7 +279,7 @@
     )(core, place, *sources)
 
 
-def dense_halves(core, own, near, far, block_cols):
+def dense_halves(core, own, near, swap, block_cols):
     row_blocks, slots = block_cols.shape
     entry = jnp.arange(slots * row_blocks)
     place = jnp.arange(row_blocks * row_blocks)
@@ -293,7 +293,9 @@
         return blocks[0].transpose(1, 0, 2).reshape(-1, BLOCK * BLOCK // 2)
 
     core = core.reshape(1)
-    return spread_blocks(60, core, chosen, flat(own)), spread_blocks(16, core, chosen, flat(near), flat(far))
+    own, near = lax.optimization_barrier((spread_blocks(60, core, chosen, flat(own)), near))
+    far = lax.ppermute(near, "wide", swap)
+    return own, spread_blocks(16, core, chosen, flat(near), flat(far))
 
 
 def other_half_pairs(wide, narrow):
@@ -318,9 +320,8 @@
     near = lax.ppermute(part, ("wide", "narrow"), other_half_pairs(wide, narrow))
     rows = functions.reshape(FUN_DEV, TILES, LANES).transpose(1, 0, 2).reshape(TILES * FUN_DEV, LANES)
     filtered = filter_twice(rows, potential, cheb_coef)
-    filtered, near = lax.optimization_barrier((filtered, near))
-    far = lax.ppermute(near, "wide", [(index, index ^ 1) for index in range(wide)])
-    mixers = dense_halves(core, kernel_halves, near, far, block_cols)
+    swap = [(index, index ^ 1) for index in range(wide)]
+    mixers = dense_halves(core, kernel_halves, near, swap, block_cols)
     outgoing = filtered.reshape(devices, own // LANES, FUN_DEV, LANES).transpose(0, 2, 1, 3)
     outgoing = outgoing.reshape(devices, FUN_DEV, own)
     points = lax.all_to_all(outgoing, ("narrow", "wide"), split_axis=0, concat_axis=0, tiled=True)

time: 78 us -> 79.4 us (1.018)
  blocking collectives: 26.9 us -> 30 us
  waiting for transfers between devices: 9.09 us -> 7.4 us
  starting transfers between devices: 18.5 us -> 19.5 us
  local copies, waits for them, and re-layouts: 2.24 us -> 1.26 us
    all_to_all x1, waiting for transfers between devices: 9.08 us -> 3.2 us  [local(): lax.all_to_all(outgoing, ('narrow', 'wide'), split_axis=0, concat_axis=0,...]
    all_to_all x1, blocking collectives: 26.9 us -> 30 us  [local(): lax.all_to_all(mixed.reshape(devices, FUN_DEV, own), ('narrow', 'wide'),...]
    ppermute x1, waiting for transfers between devices: 0.01 us -> 2.85 us  [local(): lax.ppermute(part, ('wide', 'narrow'), other_half_pairs(wide, narrow))]
    all_to_all x1, starting transfers between devices: 14.1 us -> 15.7 us  [local(): lax.all_to_all(outgoing, ('narrow', 'wide'), split_axis=0, concat_axis=0,...]
    ppermute x1, waiting for transfers between devices: 0.01 us -> 1.35 us  [dense_halves(): far = lax.ppermute(near, 'wide', swap)]
    dynamic_slice x1, local copies, waits for them, and re-layouts: 1.02 us -> 0.03 us  [local(): part = lax.dynamic_slice_in_dim(kernel_halves, core * slots, slots, 2)]
  transfers between devices with their start and end apart: 3 -> 3, of which waited for: 1 -> 3; matrix products, arithmetic and copies ran while one was open for 1% -> 1% of each run, Pallas kernels for 24% -> 10%
where the time goes in v7:
time: 79.4 us; the launch traced here: 79.2 us
  blocking collectives  30 us (38%)
  Pallas kernels  20.1 us (25%)
  starting transfers between devices  19.5 us (25%)
  waiting for transfers between devices  7.4 us (9%)
  local copies, waits for them, and re-layouts  1.26 us (2%)
  other arithmetic  0.81 us (1%)
    all_to_all x1, blocking collectives, local(): lax.all_to_all(mixed.reshape(devices, FUN_DEV, own), ('narrow', 'wide'),...  30 us
    all_to_all x1, starting transfers between devices, local(): lax.all_to_all(outgoing, ('narrow', 'wide'), split_axis=0, concat_axis=0,...  15.7 us
    pallas_call x1, Pallas kernels, filter_twice(): pl.pallas_call(filter_kernel, name='filter_twice', out_shape=jax.ShapeDty...  10.2 us
    pallas_call x2, Pallas kernels, spread_blocks(): pl.pallas_call(spread_kernel, name='spread_blocks', out_shape=jax.ShapeDt...  8.13 us
    all_to_all x1, waiting for transfers between devices, local(): lax.all_to_all(outgoing, ('narrow', 'wide'), split_axis=0, concat_axis=0,...  3.2 us
    ppermute x1, waiting for transfers between devices, local(): lax.ppermute(part, ('wide', 'narrow'), other_half_pairs(wide, narrow))  2.85 us
    ppermute x1, starting transfers between devices, dense_halves(): far = lax.ppermute(near, 'wide', swap)  2.37 us
    pallas_call x1, Pallas kernels, mix_twice(): pl.pallas_call(mix_kernel, name='mix_twice', out_shape=jax.ShapeDtypeStru...  1.73 us
  transfers between devices with their start and end apart: 3, of which 3 were waited for; matrix products, arithmetic and copies ran while one was open for 1% of the time, Pallas kernels for 10%

profile of v7, /device:TPU:1, one launch (start us, length us, event | category | flops | bytes accessed | tf_op | source)
XLA Modules:
  0.0 79.2 jit_solution(640804488911137165)
XLA Ops:
  0.0 10.2 %filter_twice.1 = bf16[2048,128]{1,0:T(8,128)(2,1)} custom-call(f32[9]{0:T(128)} %coef_hbm.1, f32[64,1024]{1,0:T(8,128)} %potential_hbm.1, bf16[2048,128]{1,0:T(8,128)(2,1)} %bitcast.36), custom_call_target="tpu_custom_call" | custom-call | flops 60000000 | bytes 40000000 | tf_op jit(solution)/shard_map/filter_twice/pallas_call | solution.py:182
  10.2 0.0 copy-start.2
  10.3 15.7 %all-to-all-start = ((bf16[256,4,256]{2,1,0:T(4,128)(2,1)}), bf16[256,4,256]{2,1,0:T(4,128)(2,1)S(1)}, u32[]{:S(2)}, u32[]{:S(2)}) async-start(bf16[256,4,256]{2,1,0:T(4,128)(2,1)} %bitcast.33), calls=%async_computation | async-start | bytes 1048576 | tf_op jit(solution)/shard_map/all_to_all | solution.py:327
  25.9 0.0 copy-done.2
  25.9 0.0 copy-start.3
  26.0 1.5 %collective-permute-start = (bf16[1,16,6,2048]{3,1,2,0:T(8,128)(2,1)S(1)}, bf16[1,16,6,2048]{3,1,2,0:T(8,128)(2,1)S(1)}, u32[]{:S(2)}, u32[]{:S(2)}) collective-permute-start(bf16[1,16,6,2048]{3,1,2,0:T(8,128)(2,1)S(1)} %constant_dynamic-slice_fusion), channel_id=1, source_target_pairs={{1,0},{32,1},{35,2},{2,3},{5,4},{36,5},{39,6},{6,7},{9,8},{40,9},{... | collective-permute-start | bytes 1179656 | tf_op jit(solution)/shard_map/ppermute | solution.py:320
  27.5 0.0 copy-done.3
  27.5 0.1 copy.8
  27.6 0.1 eq.34
  27.6 0.8 %and_convert_fusion.place_ref = bf16[256,192]{1,0:T(8,128)(2,1)} fusion(s32[192]{0:T(256)S(1)} %and_select_fusion.1, s32[192]{0:T(256)S(1)} %eq.34, s32[256]{0:T(256)S(1)} %get-tuple-element.9, s32[256]{0:T(256)S(1)} %get-tuple-element.10), kind=kLoop, calls=%fused_computation | loop fusion | flops 196608 | bytes 101888 | tf_op jit(solution)/shard_map/convert_element_type | solution.py:290
  28.4 0.0 copy-start
  28.4 5.2 %spread_blocks.2.own_ref = bf16[1024,512]{1,0:T(8,128)(2,1)} custom-call(s32[1]{0:T(128)} %bitcast.1.core_ref, bf16[256,192]{1,0:T(8,128)(2,1)} %and_convert_fusion.place_ref, bf16[192,2048]{1,0:T(8,128)(2,1)} %bitcast.35), custom_call_target="tpu_custom_call" | custom-call | flops 200000000 | bytes 8000000 | tf_op jit(solution)/shard_map/spread_blocks/pallas_call | solution.py:270
  33.6 2.9 %collective-permute-done = bf16[1,16,6,2048]{3,1,2,0:T(8,128)(2,1)S(1)} collective-permute-done((bf16[1,16,6,2048]{3,1,2,0:T(8,128)(2,1)S(1)}, bf16[1,16,6,2048]{3,1,2,0:T(8,128)(2,1)S(1)}, u32[]{:S(2)}, u32[]{:S(2)}) %collective-permute-start) | collective-permute-done | bytes 393248 | tf_op jit(solution)/shard_map/ppermute | solution.py:320
  36.5 2.4 %collective-permute-start.1 = (bf16[1,16,6,2048]{3,1,2,0:T(8,128)(2,1)S(1)}, bf16[1,16,6,2048]{3,1,2,0:T(8,128)(2,1)S(1)}, u32[]{:S(2)}, u32[]{:S(2)}) collective-permute-start(bf16[1,16,6,2048]{3,1,2,0:T(8,128)(2,1)S(1)} %collective-permute-done), channel_id=1, source_target_pairs={{0,2},{2,0},{4,6},{6,4},{8,10},{10,8},{12,14},{14,12},{16,18},{18,... | collective-permute-start | bytes 1179656 | tf_op jit(solution)/shard_map/ppermute | solution.py:297
  38.9 1.3 %collective-permute-done.1 = bf16[1,16,6,2048]{3,1,2,0:T(8,128)(2,1)S(1)} collective-permute-done((bf16[1,16,6,2048]{3,1,2,0:T(8,128)(2,1)S(1)}, bf16[1,16,6,2048]{3,1,2,0:T(8,128)(2,1)S(1)}, u32[]{:S(2)}, u32[]{:S(2)}) %collective-permute-start.1) | collective-permute-done | bytes 393248 | tf_op jit(solution)/shard_map/ppermute | solution.py:297
  40.2 0.0 copy-done
  40.2 0.0 copy-start.1
  40.2 2.9 %spread_blocks.3.other_ref = bf16[1024,512]{1,0:T(8,128)(2,1)S(1)} custom-call(s32[1]{0:T(128)} %bitcast.1.core_ref, bf16[256,192]{1,0:T(8,128)(2,1)S(1)} %copy-done, bf16[96,2048]{1,0:T(8,128)(2,1)S(1)} %bitcast.31, bf16[96,2048]{1,0:T(8,128)(2,1)S(1)} %bitcast.32), custom_call_target="tpu_custom_call" | custom-call | flops 200000000 | bytes 8000000 | tf_op jit(solution)/shard_map/spread_blocks/pallas_call | solution.py:270
  43.2 3.2 %all-to-all-done = bf16[256,4,256]{2,1,0:T(4,128)(2,1)S(1)} async-done(((bf16[256,4,256]{2,1,0:T(4,128)(2,1)}), bf16[256,4,256]{2,1,0:T(4,128)(2,1)S(1)}, u32[]{:S(2)}, u32[]{:S(2)}) %all-to-all-start) | async-done | bytes 524320 | tf_op jit(solution)/shard_map/all_to_all | solution.py:327
  46.4 0.1 reshape.113.points_ref
  46.5 0.0 copy-done.1
  46.5 1.7 %mix_twice.1 = bf16[1024,256]{1,0:T(8,128)(2,1)S(1)} custom-call(s32[1]{0:T(128)} %bitcast.half_ref, bf16[1024,512]{1,0:T(8,128)(2,1)S(1)} %copy-done.1, bf16[1024,512]{1,0:T(8,128)(2,1)S(1)} %spread_blocks.3.other_ref, bf16[1024,256]{1,0:T(8,128)(2,1)S(1)} %reshape.113.points_ref), custom_call_target="tpu_custom_call" | custom-call | flops 1100000000 | bytes 4000000 | tf_op jit(solution)/shard_map/mix_twice/pallas_call | solution.py:221
  48.2 0.1 reshape.114
  48.4 30.0 %all_to_all.10 = bf16[256,4,256]{2,1,0:T(4,128)(2,1)S(1)} all-to-all(bf16[256,4,256]{2,1,0:T(4,128)(2,1)S(1)} %reshape.114), channel_id=1, replica_groups=mesh['wide'=128,'narrow'=2] {'narrow','wide'}, dimensions={0} | all-to-all | bytes 1048576 | tf_op jit(solution)/shard_map/all_to_all | solution.py:330
  78.4 0.8 %copy.12 = bf16[4,65536]{1,0:T(4,128)(2,1)} copy(bf16[4,65536]{1,0:T(4,128)(2,1)S(1)} %bitcast.34) | data formatting | bytes 1048576
  (3 shorter events, 0.0 us)
Async XLA Ops:
  10.2 15.7 %copy-start.2 = (bf16[1,16,12,2048]{3,1,2,0:T(8,128)(2,1)S(1)}, bf16[1,16,12,2048]{3,1,2,0:T(8,128)(2,1)}, u32[]{:S(2)}) copy-start(bf16[1,16,12,2048]{3,1,2,0:T(8,128)(2,1)} %param.9) | copy-start | bytes 2359300
  10.3 36.1 %all-to-all-start = ((bf16[256,4,256]{2,1,0:T(4,128)(2,1)}), bf16[256,4,256]{2,1,0:T(4,128)(2,1)S(1)}, u32[]{:S(2)}, u32[]{:S(2)}) async-start(bf16[256,4,256]{2,1,0:T(4,128)(2,1)} %bitcast.33), calls=%async_computation | async-start | bytes 1048576 | tf_op jit(solution)/shard_map/all_to_all | solution.py:327
  25.9 1.5 %copy-start.3 = (s32[16,12]{1,0:T(8,128)S(1)}, s32[16,12]{1,0:T(8,128)}, u32[]{:S(2)}) copy-start(s32[16,12]{1,0:T(8,128)} %param.8) | copy-start | bytes 2308
  26.0 10.5 %collective-permute-start = (bf16[1,16,6,2048]{3,1,2,0:T(8,128)(2,1)S(1)}, bf16[1,16,6,2048]{3,1,2,0:T(8,128)(2,1)S(1)}, u32[]{:S(2)}, u32[]{:S(2)}) collective-permute-start(bf16[1,16,6,2048]{3,1,2,0:T(8,128)(2,1)S(1)} %constant_dynamic-slice_fusion), channel_id=1, source_target_pairs={{1,0},{32,1},{35,2},{2,3},{5,4},{36,5},{39,6},{6,7},{9,8},{40,9},{... | collective-permute-start | bytes 1179656 | tf_op jit(solution)/shard_map/ppermute | solution.py:320
  28.4 11.8 %copy-start = (bf16[256,192]{1,0:T(8,128)(2,1)S(1)}, bf16[256,192]{1,0:T(8,128)(2,1)}, u32[]{:S(2)}) copy-start(bf16[256,192]{1,0:T(8,128)(2,1)} %and_convert_fusion.place_ref) | copy-start | bytes 294916
  36.5 3.7 %collective-permute-start.1 = (bf16[1,16,6,2048]{3,1,2,0:T(8,128)(2,1)S(1)}, bf16[1,16,6,2048]{3,1,2,0:T(8,128)(2,1)S(1)}, u32[]{:S(2)}, u32[]{:S(2)}) collective-permute-start(bf16[1,16,6,2048]{3,1,2,0:T(8,128)(2,1)S(1)} %collective-permute-done), channel_id=1, source_target_pairs={{0,2},{2,0},{4,6},{6,4},{8,10},{10,8},{12,14},{14,12},{16,18},{18,... | collective-permute-start | bytes 1179656 | tf_op jit(solution)/shard_map/ppermute | solution.py:297
  40.2 6.3 %copy-start.1 = (bf16[1024,512]{1,0:T(8,128)(2,1)S(1)}, bf16[1024,512]{1,0:T(8,128)(2,1)}, u32[]{:S(2)}) copy-start(bf16[1024,512]{1,0:T(8,128)(2,1)} %spread_blocks.2.own_ref) | copy-start | bytes 3145732

commit v8 on v6

--- a/solution.py
+++ b/solution.py
@@ -210,10 +210,11 @@
     for source_ref, target_ref in ((first_ref, middle_ref), (middle_ref, out_ref)):
         own = source_ref[pl.ds(pl.multiple_of(half_ref[0] * count, count), count), :]
         other = source_ref[pl.ds(pl.multiple_of((1 - half_ref[0]) * count, count), count), :]
+        both = jnp.concatenate([own, other], 0)
         for start in range(0, FUNCS, size):
             rows = slice(start, start + size)
-            part = jnp.dot(own_ref[rows, :], own, preferred_element_type=jnp.float32)
-            part = part + jnp.dot(other_ref[rows, :], other, preferred_element_type=jnp.float32)
+            mixer = jnp.concatenate([own_ref[rows, :], other_ref[rows, :]], 1)
+            part = jnp.dot(mixer, both, preferred_element_type=jnp.float32)
             target_ref[rows, :] = part.astype(jnp.bfloat16)
 
 

time: 78 us -> 78 us (level)
  no operation moved by 1% of the time
where the time goes in v8:
time: 78 us; the launch traced here: 77.7 us
  blocking collectives  26.9 us (34%)
  Pallas kernels  20.1 us (26%)
  starting transfers between devices  18.5 us (24%)
  waiting for transfers between devices  9.09 us (12%)
  local copies, waits for them, and re-layouts  2.24 us (3%)
  other arithmetic  0.8 us (1%)
    all_to_all x1, blocking collectives, local(): lax.all_to_all(mixed.reshape(devices, FUN_DEV, own), ('narrow', 'wide'),...  26.9 us
    all_to_all x1, starting transfers between devices, local(): lax.all_to_all(outgoing, ('narrow', 'wide'), split_axis=0, concat_axis=0,...  14.1 us
    pallas_call x1, Pallas kernels, filter_twice(): pl.pallas_call(filter_kernel, name='filter_twice', out_shape=jax.ShapeDty...  10.2 us
    all_to_all x1, waiting for transfers between devices, local(): lax.all_to_all(outgoing, ('narrow', 'wide'), split_axis=0, concat_axis=0,...  9.08 us
    pallas_call x2, Pallas kernels, spread_blocks(): pl.pallas_call(spread_kernel, name='spread_blocks', out_shape=jax.ShapeDt...  8.13 us
    ppermute x1, starting transfers between devices, local(): lax.ppermute(near, 'wide', [(index, index ^ 1) for index in range(wide)])  2.23 us
    ppermute x1, starting transfers between devices, local(): lax.ppermute(part, ('wide', 'narrow'), other_half_pairs(wide, narrow))  2.2 us
    pallas_call x1, Pallas kernels, mix_twice(): pl.pallas_call(mix_kernel, name='mix_twice', out_shape=jax.ShapeDtypeStru...  1.73 us
  transfers between devices with their start and end apart: 3, of which 1 were waited for; matrix products, arithmetic and copies ran while one was open for 1% of the time, Pallas kernels for 24%

profile of v8, /device:TPU:1, one launch (start us, length us, event | category | flops | bytes accessed | tf_op | source)
XLA Modules:
  0.0 77.7 jit_solution(10432228072114952163)
XLA Ops:
  0.0 1.0 %constant_dynamic-slice_fusion = bf16[1,16,6,2048]{3,1,2,0:T(8,128)(2,1)S(1)} fusion(bf16[1,16,12,2048]{3,1,2,0:T(8,128)(2,1)} %param.9, s32[]{:T(128)S(6)} %select_n.46), kind=kLoop, calls=%fused_computation.9 | loop fusion | bytes 786436 | tf_op jit(solution)/shard_map/dynamic_slice | solution.py:318
  1.0 2.2 %collective-permute-start = (bf16[1,16,6,2048]{3,1,2,0:T(8,128)(2,1)S(1)}, bf16[1,16,6,2048]{3,1,2,0:T(8,128)(2,1)S(1)}, u32[]{:S(2)}, u32[]{:S(2)}) collective-permute-start(bf16[1,16,6,2048]{3,1,2,0:T(8,128)(2,1)S(1)} %constant_dynamic-slice_fusion), channel_id=1, source_target_pairs={{1,0},{32,1},{35,2},{2,3},{5,4},{36,5},{39,6},{6,7},{9,8},{40,9},{... | collective-permute-start | bytes 1179656 | tf_op jit(solution)/shard_map/ppermute | solution.py:319
  3.2 10.2 %filter_twice.1 = bf16[2048,128]{1,0:T(8,128)(2,1)} custom-call(f32[9]{0:T(128)} %coef_hbm.1, f32[64,1024]{1,0:T(8,128)} %potential_hbm.1, bf16[2048,128]{1,0:T(8,128)(2,1)} %bitcast.36), custom_call_target="tpu_custom_call" | custom-call | flops 60000000 | bytes 40000000 | tf_op jit(solution)/shard_map/filter_twice/pallas_call | solution.py:182
  13.5 0.0 collective-permute-done
  13.5 0.0 copy-start.2
  13.5 14.1 %all-to-all-start = ((bf16[256,4,256]{2,1,0:T(4,128)(2,1)}), bf16[256,4,256]{2,1,0:T(4,128)(2,1)S(1)}, u32[]{:S(2)}, u32[]{:S(2)}) async-start(bf16[256,4,256]{2,1,0:T(4,128)(2,1)} %bitcast.33), calls=%async_computation | async-start | bytes 1048576 | tf_op jit(solution)/shard_map/all_to_all | solution.py:327
  27.6 2.2 %collective-permute-start.1 = (bf16[1,16,6,2048]{3,1,2,0:T(8,128)(2,1)S(1)}, bf16[1,16,6,2048]{3,1,2,0:T(8,128)(2,1)S(1)}, u32[]{:S(2)}, u32[]{:S(2)}) collective-permute-start(bf16[1,16,6,2048]{3,1,2,0:T(8,128)(2,1)S(1)} %collective-permute-done), channel_id=1, source_target_pairs={{0,2},{2,0},{4,6},{6,4},{8,10},{10,8},{12,14},{14,12},{16,18},{18,... | collective-permute-start | bytes 1179656 | tf_op jit(solution)/shard_map/ppermute | solution.py:323
  29.8 0.0 copy-done.2
  29.8 0.1 copy.8
  29.9 0.1 eq.34
  30.0 0.8 %and_convert_fusion.place_ref = bf16[256,192]{1,0:T(8,128)(2,1)} fusion(s32[192]{0:T(256)S(1)} %and_select_fusion.1, s32[192]{0:T(256)S(1)} %eq.34, s32[256]{0:T(256)S(1)} %get-tuple-element.9, s32[256]{0:T(256)S(1)} %get-tuple-element.10), kind=kLoop, calls=%fused_computation | loop fusion | flops 196608 | bytes 101888 | tf_op jit(solution)/shard_map/convert_element_type | solution.py:291
  30.8 0.0 copy-start
  30.8 5.2 %spread_blocks.2.own_ref = bf16[1024,512]{1,0:T(8,128)(2,1)} custom-call(s32[1]{0:T(128)} %bitcast.1.core_ref, bf16[256,192]{1,0:T(8,128)(2,1)} %and_convert_fusion.place_ref, bf16[192,2048]{1,0:T(8,128)(2,1)} %bitcast.35), custom_call_target="tpu_custom_call" | custom-call | flops 200000000 | bytes 8000000 | tf_op jit(solution)/shard_map/spread_blocks/pallas_call | solution.py:271
  36.0 0.0 collective-permute-done.1
  36.0 0.0 copy-done
  36.0 0.0 copy-start.1
  36.0 2.9 %spread_blocks.3.other_ref = bf16[1024,512]{1,0:T(8,128)(2,1)S(1)} custom-call(s32[1]{0:T(128)} %bitcast.1.core_ref, bf16[256,192]{1,0:T(8,128)(2,1)S(1)} %copy-done, bf16[96,2048]{1,0:T(8,128)(2,1)S(1)} %bitcast.31, bf16[96,2048]{1,0:T(8,128)(2,1)S(1)} %bitcast.32), custom_call_target="tpu_custom_call" | custom-call | flops 200000000 | bytes 8000000 | tf_op jit(solution)/shard_map/spread_blocks/pallas_call | solution.py:271
  39.0 9.1 %all-to-all-done = bf16[256,4,256]{2,1,0:T(4,128)(2,1)S(1)} async-done(((bf16[256,4,256]{2,1,0:T(4,128)(2,1)}), bf16[256,4,256]{2,1,0:T(4,128)(2,1)S(1)}, u32[]{:S(2)}, u32[]{:S(2)}) %all-to-all-start) | async-done | bytes 524320 | tf_op jit(solution)/shard_map/all_to_all | solution.py:327
  48.0 0.1 reshape.113.points_ref
  48.2 0.0 copy-done.1
  48.2 1.7 %mix_twice.1 = bf16[1024,256]{1,0:T(8,128)(2,1)S(1)} custom-call(s32[1]{0:T(128)} %bitcast.half_ref, bf16[1024,512]{1,0:T(8,128)(2,1)S(1)} %copy-done.1, bf16[1024,512]{1,0:T(8,128)(2,1)S(1)} %spread_blocks.3.other_ref, bf16[1024,256]{1,0:T(8,128)(2,1)S(1)} %reshape.113.points_ref), custom_call_target="tpu_custom_call" | custom-call | flops 1100000000 | bytes 4000000 | tf_op jit(solution)/shard_map/mix_twice/pallas_call | solution.py:222
  49.9 0.1 reshape.114
  50.0 26.9 %all_to_all.10 = bf16[256,4,256]{2,1,0:T(4,128)(2,1)S(1)} all-to-all(bf16[256,4,256]{2,1,0:T(4,128)(2,1)S(1)} %reshape.114), channel_id=1, replica_groups=mesh['wide'=128,'narrow'=2] {'narrow','wide'}, dimensions={0} | all-to-all | bytes 1048576 | tf_op jit(solution)/shard_map/all_to_all | solution.py:330
  76.9 0.8 %copy.12 = bf16[4,65536]{1,0:T(4,128)(2,1)} copy(bf16[4,65536]{1,0:T(4,128)(2,1)S(1)} %bitcast.34) | data formatting | bytes 1048576
  (2 shorter events, 0.0 us)
Async XLA Ops:
  1.0 12.4 %collective-permute-start = (bf16[1,16,6,2048]{3,1,2,0:T(8,128)(2,1)S(1)}, bf16[1,16,6,2048]{3,1,2,0:T(8,128)(2,1)S(1)}, u32[]{:S(2)}, u32[]{:S(2)}) collective-permute-start(bf16[1,16,6,2048]{3,1,2,0:T(8,128)(2,1)S(1)} %constant_dynamic-slice_fusion), channel_id=1, source_target_pairs={{1,0},{32,1},{35,2},{2,3},{5,4},{36,5},{39,6},{6,7},{9,8},{40,9},{... | collective-permute-start | bytes 1179656 | tf_op jit(solution)/shard_map/ppermute | solution.py:319
  13.5 16.4 %copy-start.2 = (s32[16,12]{1,0:T(8,128)S(1)}, s32[16,12]{1,0:T(8,128)}, u32[]{:S(2)}) copy-start(s32[16,12]{1,0:T(8,128)} %param.8) | copy-start | bytes 2308
  13.5 34.6 %all-to-all-start = ((bf16[256,4,256]{2,1,0:T(4,128)(2,1)}), bf16[256,4,256]{2,1,0:T(4,128)(2,1)S(1)}, u32[]{:S(2)}, u32[]{:S(2)}) async-start(bf16[256,4,256]{2,1,0:T(4,128)(2,1)} %bitcast.33), calls=%async_computation | async-start | bytes 1048576 | tf_op jit(solution)/shard_map/all_to_all | solution.py:327
  27.6 8.4 %collective-permute-start.1 = (bf16[1,16,6,2048]{3,1,2,0:T(8,128)(2,1)S(1)}, bf16[1,16,6,2048]{3,1,2,0:T(8,128)(2,1)S(1)}, u32[]{:S(2)}, u32[]{:S(2)}) collective-permute-start(bf16[1,16,6,2048]{3,1,2,0:T(8,128)(2,1)S(1)} %collective-permute-done), channel_id=1, source_target_pairs={{0,2},{2,0},{4,6},{6,4},{8,10},{10,8},{12,14},{14,12},{16,18},{18,... | collective-permute-start | bytes 1179656 | tf_op jit(solution)/shard_map/ppermute | solution.py:323
  30.8 5.2 %copy-start = (bf16[256,192]{1,0:T(8,128)(2,1)S(1)}, bf16[256,192]{1,0:T(8,128)(2,1)}, u32[]{:S(2)}) copy-start(bf16[256,192]{1,0:T(8,128)(2,1)} %and_convert_fusion.place_ref) | copy-start | bytes 294916
  36.0 12.2 %copy-start.1 = (bf16[1024,512]{1,0:T(8,128)(2,1)S(1)}, bf16[1024,512]{1,0:T(8,128)(2,1)}, u32[]{:S(2)}) copy-start(bf16[1024,512]{1,0:T(8,128)(2,1)} %spread_blocks.2.own_ref) | copy-start | bytes 3145732
